TPU v7x, 128 devices: a whole 4x4x4 slice. The times are simulated.
128 devices in a mesh: ctx: 4 (over x), head: 32 (over z, y, core).
Axes of the slice: x: 4, y: 4, z: 4, core: 2. Of those that a mesh axis runs over, the one named last changes fastest.
Arguments:
- prefix_x: bfloat16 [4, 1536, 16384], P(None, 'ctx', 'head'), may hold values from -6 to 6
- prefix_bc: bfloat16 [4, 1536, 2048], P(None, 'ctx', 'head'), may hold values from -6 to 6
- prefix_gate: bfloat16 [4, 1536, 16384], P(None, 'ctx', 'head'), may hold values from -6 to 6
- prefix_steps: float32 [4, 1536, 256], P(None, 'ctx', 'head'), may hold values from -4 to 4
- x_kernel: bfloat16 [4, 16384], P(None, 'head'), may hold values from -3 to 3
- bc_kernel: bfloat16 [4, 2048], P(None, 'head'), may hold values from -3 to 3
- step_bias: float32 [256], P('head'), may hold values from -3 to -1
- log_rate: float32 [256], P('head'), may hold values from -6.2 to -1.4
- skip_gain: float32 [256], P('head'), may hold values from 0.5 to 1.5
- norm_gain: float32 [16384], replicated, may hold values from 0.5 to 1.5
- option_x: bfloat16 [16, 256, 16384], P('ctx', None, 'head'), may hold values from -6 to 6
- option_bc: bfloat16 [16, 256, 2048], P('ctx', None, 'head'), may hold values from -6 to 6
- option_gate: bfloat16 [16, 256, 16384], P('ctx', None, 'head'), may hold values from -6 to 6
- option_steps: float32 [16, 256, 256], P('ctx', None, 'head'), may hold values from -4 to 4
- option_len: int32 [16], P('ctx'), may hold values from 64 to 256, as said below
Outputs:
- prefix_out: bfloat16 [4, 1536, 16384], P(None, ('ctx', 'head'))
- option_out: bfloat16 [16, 256, 16384], P('ctx', 'head')
Inputs may be any that keep to these rules, and one draw needn't show every extreme that they name: `option_len`: some option has the full length 256 in every draw.
All inputs are finite; a program needn't handle non-finite values.
Results may differ from a plain program's by a relative error of at most 0.0051.
Values may be sent and summed in bfloat16 or wider, within the bound.
A program may use at most 128 MiB of HBM per device.

v0:
```python
import jax
import jax.numpy as jnp
from jax import lax
from jax.sharding import PartitionSpec as P

NS = 128
GROUPS = 8
INNER = 16384
OPTS = 4
BLK = 384


epsilon = 1e-05
highest = lax.Precision.HIGHEST


def swapped(block, axis, distance):
    count = lax.axis_size(axis)
    route = []
    for low in range(count):
        high = low | 1 << distance
        if high != low and high < count:
            route += [(low, high), (high, low)]
    return lax.ppermute(block, axis, route)


def from_behind(value, axis, by):
    devices = lax.axis_size(axis)
    pairs = [(i, i + by) for i in range(devices) if 0 <= i + by < devices]
    return lax.ppermute(value, axis, pairs)


def prefix(part, axis, combine, identity):
    place = lax.axis_index(axis)
    gathered = jax.tree.map(lambda a: lax.all_gather(a, axis), part)
    state = jax.tree.map(lambda a, e: jnp.zeros_like(a) + jnp.asarray(e, a.dtype), part, identity)

    def one(lap, state):
        return combine(
            state, jax.tree.map(lambda a: lax.dynamic_index_in_dim(a, lap, 0, False), gathered)
        )

    return lax.fori_loop(0, place, one, state)


def spread(block, axis, source):
    block = jnp.where(lax.axis_index(axis) == source, block, jnp.zeros_like(block))
    return lax.psum(block, axis)


def causal_conv(sequence, kernel, context):
    length = sequence.shape[1]
    joined = jnp.concatenate([context, sequence], axis=1).astype(jnp.float32)
    weights = kernel.astype(jnp.float32)
    summed = joined[:, 0:length] * weights[0]
    for offset in range(1, weights.shape[0]):
        summed = summed + joined[:, offset : offset + length] * weights[offset]
    return jax.nn.silu(summed).astype(jnp.bfloat16)


def scan_block(carry_state, pieces, decay_rate, skip_gain):
    values_low, b_rows, c_rows, step_size = pieces
    extent, heads_here = step_size.shape
    cumul = jnp.cumsum(step_size * decay_rate, axis=0)
    lower = lax.broadcasted_iota(jnp.int32, (extent, extent), 0) >= lax.broadcasted_iota(
        jnp.int32, (extent, extent), 1
    )
    ordered = cumul.T
    spans = ordered[:, :, None] - ordered[:, None, :]
    decays = jnp.exp(jnp.where(lower, spans, -jnp.inf))
    scores = jnp.einsum("tn,sn->ts", c_rows, b_rows, preferred_element_type=jnp.float32)
    weights = decays * scores[None] * step_size.T[:, None, :]
    values = values_low.astype(jnp.float32).reshape(extent, heads_here, -1)
    within = jnp.einsum("hts,shp->thp", weights, values, precision=highest)
    carried = jnp.einsum("tn,hpn->thp", c_rows.astype(jnp.float32), carry_state, precision=highest)
    carried = carried * jnp.exp(cumul)[:, :, None]
    outputs = within + carried + skip_gain[:, None] * values
    remain = jnp.exp(cumul[-1:] - cumul) * step_size
    fresh = jnp.einsum(
        "shp,sn->hpn", values * remain[:, :, None], b_rows.astype(jnp.float32), precision=highest
    )
    new_state = jnp.exp(cumul[-1])[:, None, None] * carry_state + fresh
    return (new_state, outputs.reshape(extent, -1))


def run_stretch(start_state, pieces, decay_rate, skip_gain, block_rows):
    length = pieces[0].shape[0]
    count = length // block_rows

    def cut(array):
        return array.reshape((count, block_rows) + array.shape[1:])

    def advance(state_now, piece):
        return scan_block(state_now, piece, decay_rate, skip_gain)

    final_state, outputs = lax.scan(advance, start_state, tuple((cut(array) for array in pieces)))
    return (final_state, outputs.reshape(length, -1))


def gated_norm(values, gates, gain):
    mixed = values.astype(jnp.float32) * jax.nn.silu(gates.astype(jnp.float32))
    grouped = mixed.reshape(mixed.shape[:-1] + (GROUPS, INNER // GROUPS))
    scale = lax.rsqrt(jnp.mean(grouped * grouped, axis=-1, keepdims=True) + epsilon)
    return (grouped * scale).reshape(mixed.shape) * gain


def combine(earlier, later):
    return (earlier[0] * later[0], later[0][:, :, None, None] * earlier[1] + later[1])


def per_device(
    prefix_x,
    prefix_bc,
    prefix_gate,
    prefix_steps,
    x_kernel,
    bc_kernel,
    step_bias,
    log_rate,
    skip_gain,
    norm_gain,
    option_x,
    option_bc,
    option_gate,
    option_steps,
    option_len,
):
    ctx_count = lax.axis_size("ctx")
    head_count = lax.axis_size("head")
    ctx_index = lax.axis_index("ctx")
    head_index = lax.axis_index("head")
    seqs_here, tokens, channels = prefix_x.shape
    heads_here = prefix_steps.shape[2]
    opt_here, opt_rows = (option_x.shape[0], option_x.shape[1])
    tap_count = x_kernel.shape[0] - 1
    levels = (head_count // GROUPS).bit_length() - 1
    column_count = prefix_bc.shape[2]
    prefix_rows = seqs_here * tokens
    option_rows = opt_here * opt_rows
    stacked = jnp.concatenate(
        [prefix_bc.reshape(-1, column_count), option_bc.reshape(-1, column_count), bc_kernel],
        axis=0,
    )
    for level in range(levels):
        partner = swapped(stacked, "head", level)
        lowest = head_index // (1 << level) % 2 == 0
        stacked = jnp.where(
            lowest,
            jnp.concatenate([stacked, partner], axis=1),
            jnp.concatenate([partner, stacked], axis=1),
        )
    joined_width = stacked.shape[1]
    prefix_group = stacked[:prefix_rows].reshape(seqs_here, tokens, joined_width)
    option_group = stacked[prefix_rows : prefix_rows + option_rows].reshape(
        opt_here, opt_rows, joined_width
    )
    group_kernel = stacked[prefix_rows + option_rows :]
    rims = jnp.concatenate(
        [prefix_x[:, tokens - tap_count :], prefix_group[:, tokens - tap_count :]], axis=2
    )
    before = from_behind(rims, "ctx", 1)
    x_conv = causal_conv(prefix_x, x_kernel, before[:, :, :channels])
    bc_conv = causal_conv(prefix_group, group_kernel, before[:, :, channels:])
    decay_rate = -jnp.exp(log_rate)
    step_size = jax.nn.softplus(prefix_steps + step_bias)
    zero_state = jnp.zeros((heads_here, channels // heads_here, NS), jnp.float32)

    def prompt_work(items):
        return run_stretch(zero_state, items, decay_rate, skip_gain, BLK)

    local_end, y_zero = lax.map(
        prompt_work, (x_conv, bc_conv[..., :NS], bc_conv[..., NS:], step_size)
    )
    stretch_cumul = jnp.cumsum(step_size * decay_rate, axis=1)
    local_decay = jnp.exp(stretch_cumul[:, -1])
    identity = (jnp.ones_like(local_decay), jnp.zeros_like(local_end))
    rims_wide = rims.astype(jnp.float32)
    entering = prefix((local_decay, local_end), "ctx", combine, identity)
    incoming = entering[1]
    finishing = combine(entering, (local_decay, local_end))[1]
    packed = jnp.concatenate([finishing.reshape(-1), rims_wide.reshape(-1)])
    shared = spread(packed, "ctx", ctx_count - 1)
    state_count = finishing.size
    final_state = shared[:state_count].reshape(finishing.shape)
    last_rims = shared[state_count:].reshape(rims_wide.shape)
    last_rims = last_rims.astype(jnp.bfloat16)
    carried = jnp.einsum(
        "sln,shpn->slhp", bc_conv[..., NS:].astype(jnp.float32), incoming, precision=highest
    )
    carried = carried * jnp.exp(stretch_cumul)[..., None]
    y_prefix = (y_zero + carried.reshape(seqs_here, tokens, channels)).astype(jnp.bfloat16)
    owners = (ctx_index * opt_here + jnp.arange(opt_here, dtype=jnp.int32)) // OPTS
    option_start = jnp.take(final_state, owners, axis=0)
    option_rims = jnp.take(last_rims, owners, axis=0)
    option_x_conv = causal_conv(option_x, x_kernel, option_rims[:, :, :channels])
    option_bc_conv = causal_conv(option_group, group_kernel, option_rims[:, :, channels:])
    option_size = jax.nn.softplus(option_steps + step_bias)

    def option_work(items):
        ignored, outputs = run_stretch(items[0], items[1:], decay_rate, skip_gain, opt_rows)
        return outputs

    y_option = lax.map(
        option_work,
        (
            option_start,
            option_x_conv,
            option_bc_conv[..., :NS],
            option_bc_conv[..., NS:],
            option_size,
        ),
    )
    y_option = y_option.astype(jnp.bfloat16)
    prefix_y, prefix_z, option_y, option_z = (
        lax.all_to_all(y_prefix, "head", split_axis=1, concat_axis=2, tiled=True),
        lax.all_to_all(prefix_gate, "head", split_axis=1, concat_axis=2, tiled=True),
        lax.all_to_all(y_option, "head", split_axis=1, concat_axis=2, tiled=True),
        lax.all_to_all(option_gate, "head", split_axis=1, concat_axis=2, tiled=True),
    )
    prefix_out = gated_norm(prefix_y, prefix_z, norm_gain).astype(jnp.bfloat16)
    rows_here = option_y.shape[1]
    positions = head_index * rows_here + lax.broadcasted_iota(jnp.int32, (opt_here, rows_here), 1)
    keep = (positions < option_len[:, None]).astype(jnp.float32)[..., None]
    option_out = (gated_norm(option_y, option_z, norm_gain) * keep).astype(jnp.bfloat16)
    return (prefix_out, option_out)


def solution(mesh):
    in_specs = (
        P(None, "ctx", "head"),
        P(None, "ctx", "head"),
        P(None, "ctx", "head"),
        P(None, "ctx", "head"),
        P(None, "head"),
        P(None, "head"),
        P("head"),
        P("head"),
        P("head"),
        P(),
        P("ctx", None, "head"),
        P("ctx", None, "head"),
        P("ctx", None, "head"),
        P("ctx", None, "head"),
        P("ctx"),
    )
    out_specs = (P(None, ("ctx", "head"), None), P("ctx", "head", None))
    return jax.shard_map(
        per_device, mesh=mesh, in_specs=in_specs, out_specs=out_specs, check_vma=False
    )
```

profile of v0, /device:TPU:1, one launch (start us, length us, event | category | flops | bytes accessed | tf_op | source)
XLA Modules:
  0.0 326.3 jit_solution(13158080142795562834)
XLA Ops:
  9.9 1.5 collective-permute-start
  12.2 1.9 copy.126
  17.5 13.7 %collective-permute-done.1 = bf16[2564,128]{1,0:T(8,128)(2,1)} collective-permute-done((bf16[2564,128]{1,0:T(8,128)(2,1)S(1)}, bf16[2564,128]{1,0:T(8,128)(2,1)}, u32[]{:S(2)}, u32[]{:S(2)}) %collective-permute-start.1) | collective-permute-done | bytes 656416 | tf_op jit(solution)/shard_map/ppermute | solution.py:24
  34.3 3.4 %collective-permute-start.2 = (bf16[4,3,768]{2,1,0:T(4,128)(2,1)S(1)}, bf16[4,3,768]{2,1,0:T(4,128)(2,1)S(1)}, u32[]{:S(2)}, u32[]{:S(2)}) collective-permute-start(bf16[4,3,768]{2,1,0:T(4,128)(2,1)S(1)} %get-tuple-element.266), channel_id=1, source_target_pairs={{0,32},{32,64},{64,96},{1,33},{33,65},{65,97},{2,34},{34,66},{66,9... | collective-permute-start | bytes 55304 | tf_op jit(solution)/shard_map/ppermute | solution.py:30
  42.9 3.9 %multiply_convert_fusion.1 = bf16[4,384,512]{1,2,0:T(8,128)(2,1)} fusion(f32[4,387,512]{1,2,0:T(8,128)S(1)} %maximum_convert_fusion, f32[512]{0:T(512)S(1)} %bitcast.294, f32[512]{0:T(512)S(1)} %bitcast.292, f32[512]{0:T(512)S(1)} %bitcast.290, f32[512]{0:T(512)S(1)} %bitcast.288), kind=kLoop, calls=%fused_computation.109 | loop fusion | flops 9437184 | bytes 14163968 | tf_op jit(solution)/shard_map/convert_element_type | solution.py:58
  46.9 52.9 %while.30 = (s32[]{:T(128)}, f32[4,8,64,128]{3,2,1,0:T(8,128)S(1)}, f32[4,384,512]{2,1,0:T(8,128)}, f32[4,384,8]{1,2,0:T(8,128)S(1)}, f32[8]{0:T(128)}, /*index=...) while((s32[]{:T(128)}, f32[4,8,64,128]{3,2,1,0:T(8,128)S(1)}, ...), condition=%wide.region_3.4_spmd, body=%wide.region_0.3_spmd.sunk | while | flops 1554411520 | bytes 11007041 | solution.py:171
  51.5 3.9 %fusion.144 = f32[384,8,64]{0,2,1:T(8,128)S(1)} fusion(bf16[384,8,64]{0,2,1:T(8,128)(2,1)S(1)} %bitcast.259, f32[8,384]{1,0:T(8,128)S(1)} %dynamic-slice_bitcast_fusion.6, f32[384,384]{1,0:T(8,128)S(1)} %fusion.143, f32[8,384]{1,0:T(8,128)S(1)} %add_bitcast_fusion.8, pred[384,384]{1,0:T(8,128)(4,1)S(1)} %iota_compare_fusion.4), kind=kOutput, calls=%fused_computation.16.clone.1 | convolution fusion | flops 910688256 | bytes 1941504 | tf_op jit(solution)/shard_map/while/body/eval_jaxpr/while/body/eval_jaxpr/hts,shp->thp/dot_general | solution.py:74
  55.4 1.5 fusion.145
  64.7 3.9 %fusion.144 = f32[384,8,64]{0,2,1:T(8,128)S(1)} fusion(bf16[384,8,64]{0,2,1:T(8,128)(2,1)S(1)} %bitcast.259, f32[8,384]{1,0:T(8,128)S(1)} %dynamic-slice_bitcast_fusion.6, f32[384,384]{1,0:T(8,128)S(1)} %fusion.143, f32[8,384]{1,0:T(8,128)S(1)} %add_bitcast_fusion.8, pred[384,384]{1,0:T(8,128)(4,1)S(1)} %iota_compare_fusion.4), kind=kOutput, calls=%fused_computation.16.clone.1 | convolution fusion | flops 910688256 | bytes 1941504 | tf_op jit(solution)/shard_map/while/body/eval_jaxpr/while/body/eval_jaxpr/hts,shp->thp/dot_general | solution.py:74
  68.6 1.5 fusion.145
  77.9 3.9 %fusion.144 = f32[384,8,64]{0,2,1:T(8,128)S(1)} fusion(bf16[384,8,64]{0,2,1:T(8,128)(2,1)S(1)} %bitcast.259, f32[8,384]{1,0:T(8,128)S(1)} %dynamic-slice_bitcast_fusion.6, f32[384,384]{1,0:T(8,128)S(1)} %fusion.143, f32[8,384]{1,0:T(8,128)S(1)} %add_bitcast_fusion.8, pred[384,384]{1,0:T(8,128)(4,1)S(1)} %iota_compare_fusion.4), kind=kOutput, calls=%fused_computation.16.clone.1 | convolution fusion | flops 910688256 | bytes 1941504 | tf_op jit(solution)/shard_map/while/body/eval_jaxpr/while/body/eval_jaxpr/hts,shp->thp/dot_general | solution.py:74
  91.2 3.9 %fusion.144 = f32[384,8,64]{0,2,1:T(8,128)S(1)} fusion(bf16[384,8,64]{0,2,1:T(8,128)(2,1)S(1)} %bitcast.259, f32[8,384]{1,0:T(8,128)S(1)} %dynamic-slice_bitcast_fusion.6, f32[384,384]{1,0:T(8,128)S(1)} %fusion.143, f32[8,384]{1,0:T(8,128)S(1)} %add_bitcast_fusion.8, pred[384,384]{1,0:T(8,128)(4,1)S(1)} %iota_compare_fusion.4), kind=kOutput, calls=%fused_computation.16.clone.1 | convolution fusion | flops 910688256 | bytes 1941504 | tf_op jit(solution)/shard_map/while/body/eval_jaxpr/while/body/eval_jaxpr/hts,shp->thp/dot_general | solution.py:74
  100.8 3.1 copy.143
  103.9 9.8 %all-to-all-start.3 = ((bf16[4,256,512]{2,0,1:T(4,128)(2,1)}), bf16[4,256,512]{2,0,1:T(4,128)(2,1)S(1)}, u32[]{:S(2)}, u32[]{:S(2)}) async-start(bf16[4,256,512]{2,0,1:T(4,128)(2,1)} %copy.143), calls=%async_computation.3 | async-start | bytes 2097152 | tf_op jit(solution)/shard_map/all_to_all | solution.py:218
  113.7 3.4 %reduce-window.22 = f32[4,8,3,128]{3,1,2,0:T(8,128)S(1)} reduce-window(f32[4,8,3,128]{3,1,2,0:T(8,128)S(1)} %get-tuple-element.257, f32[]{:T(128)} %constant.203.clone.1), window={size=1x1x1x128 pad=0_0x0_0x0_0x127_0}, to_apply=%region_4.5 | reduce-window | flops 1560576 | bytes 98308 | tf_op jit(solution)/shard_map/reduce-window.4
  119.1 3.8 %copy.134 = bf16[4,384,512]{2,0,1:T(4,128)(2,1)} copy(bf16[4,384,512]{2,1,0:T(8,128)(2,1)} %param.23) | data formatting | bytes 3145728 | tf_op args[2]
  122.9 10.3 %all-gather = f32[16,1,8]{2,1,0:T(1,128)S(1)} all-gather(f32[4,1,8]{2,1,0:T(1,128)S(1)} %copy.129), channel_id=2, replica_groups=mesh['ctx'=4,'head'=32] {'ctx'}, dimensions={0}, use_global_device_ids=true | all-gather | bytes 640 | tf_op jit(solution)/shard_map/all_gather | solution.py:35
  133.7 9.0 %all-to-all-start.1 = ((bf16[4,384,512]{2,0,1:T(4,128)(2,1)}), bf16[4,384,512]{2,0,1:T(4,128)(2,1)S(1)}, u32[]{:S(2)}, u32[]{:S(2)}) async-start(bf16[4,384,512]{2,0,1:T(4,128)(2,1)} %copy.134), calls=%async_computation.1 | async-start | bytes 3145728 | tf_op jit(solution)/shard_map/all_to_all | solution.py:216
  142.8 1.6 bitcast_convert_fusion.1
  144.4 9.1 %all-gather.4.cloned.1.call-done = f32[16,8,64,128]{3,2,1,0:T(8,128)} async-done(((f32[4,8,64,128]{3,2,1,0:T(8,128)}), f32[16,8,64,128]{3,2,1,0:T(8,128)}) %all-gather.4.cloned.1.call-update) | async-done | bytes 4194320 | tf_op jit(solution)/shard_map/all_gather | solution.py:35
  156.1 8.8 %all-to-all-done.1 = bf16[4,384,512]{2,0,1:T(4,128)(2,1)S(1)} async-done(((bf16[4,384,512]{2,0,1:T(4,128)(2,1)}), bf16[4,384,512]{2,0,1:T(4,128)(2,1)S(1)}, u32[]{:S(2)}, u32[]{:S(2)}) %all-to-all-start.1) | async-done | bytes 1572896 | tf_op jit(solution)/shard_map/all_to_all | solution.py:216
  165.4 2.5 copy.161
  167.8 3.0 convolution_multiply_fusion.2
  170.9 3.5 %copy.131 = f32[4,384,512]{2,1,0:T(8,128)} copy(f32[4,384,512]{1,2,0:T(8,128)} %bitcast.266) | data formatting | bytes 6291456 | tf_op jit(solution)/shard_map/reshape | solution.py:191
  174.4 3.5 %add_convert_fusion = bf16[4,384,512]{2,1,0:T(8,128)(2,1)S(1)} fusion(f32[4,384,512]{2,1,0:T(8,128)} %get-tuple-element.195, f32[4,384,512]{2,1,0:T(8,128)} %copy.131), kind=kLoop, calls=%fused_computation.108 | loop fusion | flops 1572864 | bytes 7864320 | tf_op jit(solution)/shard_map/convert_element_type | solution.py:191
  177.9 2.4 copy.132
  180.3 6.3 %all-to-all-start = ((bf16[4,384,512]{2,0,1:T(4,128)(2,1)}), bf16[4,384,512]{2,0,1:T(4,128)(2,1)}, u32[]{:S(2)}, u32[]{:S(2)}) async-start(bf16[4,384,512]{2,0,1:T(4,128)(2,1)} %copy.132), calls=%async_computation | async-start | bytes 3145728 | tf_op jit(solution)/shard_map/all_to_all | solution.py:215
  186.6 18.8 %all-reduce.2.cloned.1.call-done = f32[271360]{0:T(1024)} async-done(((f32[271360]{0:T(1024)}), f32[271360]{0:T(1024)}) %all-reduce.2.cloned.1.call-update) | async-done | bytes 1085456 | tf_op jit(solution)/shard_map/psum | solution.py:48
  209.6 2.9 multiply_convert_fusion.3
  213.8 1.6 gather_fusion.1
  216.8 68.9 %while.32 = (s32[]{:T(128)}, bf16[4,256,512]{2,0,1:T(4,128)(2,1)}, bf16[4,256,512]{1,2,0:T(8,128)(2,1)}, f32[4,256,8]{1,2,0:T(8,128)S(1)}, f32[8]{0:T(128)}, /*i...) while((s32[]{:T(128)}, bf16[4,256,512]{2,0,1:T(4,128)(2,1)}, ...), condition=%wide.region_14.15_spmd, body=%wide.region_11.14_spmd.sunk | while | flops 623970304 | bytes 4623501 | solution.py:203
  220.4 1.7 fusion.154
  223.8 10.2 %dynamic_update_slice.25 = bf16[4,256,512]{2,0,1:T(4,128)(2,1)} dynamic-update-slice(bf16[4,256,512]{2,0,1:T(4,128)(2,1)} %get-tuple-element.495, bf16[1,256,512]{2,0,1:T(2,128)(2,1)S(1)} %copy.171, s32[]{:T(128)} %get-tuple-element.494, s32[]{:T(128)} %constant.202.clone.1..sunk.1, s32[]{:T(128)} %constant.202.clone.1..sunk.1) | dynamic-update-slice | bytes 524292 | tf_op jit(solution)/shard_map/while/body/jit(dynamic_update_index_in_dim)/dynamic_update_slice | solution.py:203
  237.7 1.7 fusion.154
  241.1 10.2 %dynamic_update_slice.25 = bf16[4,256,512]{2,0,1:T(4,128)(2,1)} dynamic-update-slice(bf16[4,256,512]{2,0,1:T(4,128)(2,1)} %get-tuple-element.495, bf16[1,256,512]{2,0,1:T(2,128)(2,1)S(1)} %copy.171, s32[]{:T(128)} %get-tuple-element.494, s32[]{:T(128)} %constant.202.clone.1..sunk.1, s32[]{:T(128)} %constant.202.clone.1..sunk.1) | dynamic-update-slice | bytes 524292 | tf_op jit(solution)/shard_map/while/body/jit(dynamic_update_index_in_dim)/dynamic_update_slice | solution.py:203
  254.9 1.7 fusion.154
  258.3 10.2 %dynamic_update_slice.25 = bf16[4,256,512]{2,0,1:T(4,128)(2,1)} dynamic-update-slice(bf16[4,256,512]{2,0,1:T(4,128)(2,1)} %get-tuple-element.495, bf16[1,256,512]{2,0,1:T(2,128)(2,1)S(1)} %copy.171, s32[]{:T(128)} %get-tuple-element.494, s32[]{:T(128)} %constant.202.clone.1..sunk.1, s32[]{:T(128)} %constant.202.clone.1..sunk.1) | dynamic-update-slice | bytes 524292 | tf_op jit(solution)/shard_map/while/body/jit(dynamic_update_index_in_dim)/dynamic_update_slice | solution.py:203
  272.1 1.7 fusion.154
  275.5 10.2 %dynamic_update_slice.25 = bf16[4,256,512]{2,0,1:T(4,128)(2,1)} dynamic-update-slice(bf16[4,256,512]{2,0,1:T(4,128)(2,1)} %get-tuple-element.495, bf16[1,256,512]{2,0,1:T(2,128)(2,1)S(1)} %copy.171, s32[]{:T(128)} %get-tuple-element.494, s32[]{:T(128)} %constant.202.clone.1..sunk.1, s32[]{:T(128)} %constant.202.clone.1..sunk.1) | dynamic-update-slice | bytes 524292 | tf_op jit(solution)/shard_map/while/body/jit(dynamic_update_index_in_dim)/dynamic_update_slice | solution.py:203
  285.7 8.9 %all-to-all-start.2 = ((bf16[4,256,512]{2,0,1:T(4,128)(2,1)}), bf16[4,256,512]{2,0,1:T(4,128)(2,1)}, u32[]{:S(2)}, u32[]{:S(2)}) async-start(bf16[4,256,512]{2,0,1:T(4,128)(2,1)} %get-tuple-element.198), calls=%async_computation.2 | async-start | bytes 2097152 | tf_op jit(solution)/shard_map/all_to_all | solution.py:217
  294.6 3.7 %fusion.76 = f32[4,12,32]{0,1,2:T(8,128)S(1)} fusion(bf16[4,32,12,512]{3,0,2,1:T(4,128)(2,1)S(1)} %bitcast.265, bf16[4,32,12,512]{3,0,2,1:T(4,128)(2,1)} %bitcast.52), kind=kLoop, calls=%fused_computation.110 | loop fusion | flops 7076352 | bytes 3151872 | tf_op jit(solution)/shard_map/reduce_sum | solution.py:103
  298.3 1.9 convert_bitcast_fusion.2
  300.5 1.9 mul.500
  302.4 5.3 %mul.501 = f32[4,12,16384]{2,0,1:T(4,128)} reshape(f32[4,12,8,2048]{3,2,0,1:T(8,128)} %mul.500) | data formatting | bytes 6291456 | tf_op jit(solution)/shard_map/mul | solution.py:104
  310.5 3.2 multiply_convert_fusion
  313.7 2.1 fusion.82
  315.9 1.7 bitcast_convert_fusion
  317.8 1.7 multiply_convert_fusion.2
  (276 shorter events, 86.7 us)
Async XLA Ops:
  7.2 146.3 %all-gather.4.cloned.1.call-start = ((), (), s32[]{:S(2)}) async-start(), calls=%async_computation.5 | async-start | bytes 5242880 | tf_op jit(solution)/shard_map/all_gather | solution.py:35
  9.9 4.3 %collective-permute-start = (bf16[2564,64]{0,1:T(8,128)(2,1)S(1)}, bf16[2564,64]{0,1:T(8,128)(2,1)S(1)}, u32[]{:S(2)}, u32[]{:S(2)}) collective-permute-start(bf16[2564,64]{0,1:T(8,128)(2,1)S(1)} %pad_maximum_fusion), channel_id=1, source_target_pairs={{0,1},{1,0},{2,3},{3,2},{4,5},{5,4},{6,7},{7,6},{8,9},{9,8},{10,11... | collective-permute-start | bytes 984584 | tf_op jit(solution)/shard_map/ppermute | solution.py:24
  14.1 2.0 copy-start.35
  14.1 2.6 copy-start.23
  14.1 2.6 copy-start.13
  14.1 2.6 copy-start.32
  14.6 16.5 %collective-permute-start.1 = (bf16[2564,128]{1,0:T(8,128)(2,1)S(1)}, bf16[2564,128]{1,0:T(8,128)(2,1)}, u32[]{:S(2)}, u32[]{:S(2)}) collective-permute-start(bf16[2564,128]{1,0:T(8,128)(2,1)S(1)} %copy.121), channel_id=1, source_target_pairs={{0,2},{2,0},{1,3},{3,1},{4,6},{6,4},{5,7},{7,5},{8,10},{10,8},{9,1... | collective-permute-start | bytes 1969160 | tf_op jit(solution)/shard_map/ppermute | solution.py:24
  16.7 26.2 %copy-start.15 = (f32[1,512]{1,0:T(1,128)}, f32[1,512]{1,0:T(1,128)S(1)}, u32[]{:S(2)}) copy-start(f32[1,512]{1,0:T(1,128)S(1)} %get-tuple-element.267) | copy-start | bytes 6148
  16.7 26.2 %copy-start.17 = (f32[1,512]{1,0:T(1,128)}, f32[1,512]{1,0:T(1,128)S(1)}, u32[]{:S(2)}) copy-start(f32[1,512]{1,0:T(1,128)S(1)} %get-tuple-element.268) | copy-start | bytes 6148
  16.7 26.2 %copy-start.19 = (f32[1,512]{1,0:T(1,128)}, f32[1,512]{1,0:T(1,128)S(1)}, u32[]{:S(2)}) copy-start(f32[1,512]{1,0:T(1,128)S(1)} %get-tuple-element.269) | copy-start | bytes 6148
  16.7 26.2 %copy-start.21 = (f32[1,512]{1,0:T(1,128)}, f32[1,512]{1,0:T(1,128)S(1)}, u32[]{:S(2)}) copy-start(f32[1,512]{1,0:T(1,128)S(1)} %get-tuple-element.270) | copy-start | bytes 6148
  32.9 1.1 copy-start.6
  34.3 4.1 %collective-permute-start.2 = (bf16[4,3,768]{2,1,0:T(4,128)(2,1)S(1)}, bf16[4,3,768]{2,1,0:T(4,128)(2,1)S(1)}, u32[]{:S(2)}, u32[]{:S(2)}) collective-permute-start(bf16[4,3,768]{2,1,0:T(4,128)(2,1)S(1)} %get-tuple-element.266), channel_id=1, source_target_pairs={{0,32},{32,64},{64,96},{1,33},{33,65},{65,97},{2,34},{34,66},{66,9... | collective-permute-start | bytes 55304 | tf_op jit(solution)/shard_map/ppermute | solution.py:30
  38.0 1.5 copy-start.24
  38.1 1.5 copy-start.26
  38.1 1.5 copy-start.28
  38.1 1.5 copy-start.30
  39.6 0.9 copy-start.7
  48.9 2.5 copy-start.12
  62.1 2.5 copy-start.12
  75.4 2.5 copy-start.12
  88.6 2.5 copy-start.12
  99.8 1.0 copy-start.4
  100.8 16.9 %copy-start.10 = (bf16[4,256,512]{2,1,0:T(8,128)(2,1)S(1)}, bf16[4,256,512]{2,1,0:T(8,128)(2,1)}, u32[]{:S(2)}) copy-start(bf16[4,256,512]{2,1,0:T(8,128)(2,1)} %param.31) | copy-start | bytes 3145732
  103.9 29.8 %all-to-all-start.3 = ((bf16[4,256,512]{2,0,1:T(4,128)(2,1)}), bf16[4,256,512]{2,0,1:T(4,128)(2,1)S(1)}, u32[]{:S(2)}, u32[]{:S(2)}) async-start(bf16[4,256,512]{2,0,1:T(4,128)(2,1)} %copy.143), calls=%async_computation.3 | async-start | bytes 2097152 | tf_op jit(solution)/shard_map/all_to_all | solution.py:218
  119.1 14.2 %copy-start.34 = (s32[4]{0:T(128)S(1)}, s32[4]{0:T(128)}, u32[]{:S(2)}) copy-start(s32[4]{0:T(128)} %param.35) | copy-start | bytes 52
  119.1 14.3 %copy-start.14 = (f32[4,256,8]{1,2,0:T(8,128)S(1)}, f32[4,256,8]{1,2,0:T(8,128)}, u32[]{:S(2)}) copy-start(f32[4,256,8]{1,2,0:T(8,128)} %param.34) | copy-start | bytes 98308
  119.1 14.3 %copy-start.33 = (f32[8]{0:T(128)S(1)}, f32[8]{0:T(128)}, u32[]{:S(2)}) copy-start(f32[8]{0:T(128)} %param.27) | copy-start | bytes 100
  119.1 14.4 %slice-start = ((bf16[2564,256]{0,1:T(8,128)(2,1)}), bf16[1024,256]{0,1:T(8,128)(2,1)S(1)}, s32[]{:S(2)}) async-start(bf16[2564,256]{0,1:T(8,128)(2,1)} %copy-done.6), calls=%async_computation.6 | async-start | bytes 1048576 | tf_op jit(solution)/shard_map/slice | solution.py:154
  133.7 10.7 %copy-start.2 = (bf16[4,256,512]{2,0,1:T(4,128)(2,1)}, bf16[4,256,512]{2,0,1:T(4,128)(2,1)S(1)}, u32[]{:S(2)}) copy-start(bf16[4,256,512]{2,0,1:T(4,128)(2,1)S(1)} %all-to-all-done.3) | copy-start | bytes 3145732
  133.7 31.2 %all-to-all-start.1 = ((bf16[4,384,512]{2,0,1:T(4,128)(2,1)}), bf16[4,384,512]{2,0,1:T(4,128)(2,1)S(1)}, u32[]{:S(2)}, u32[]{:S(2)}) async-start(bf16[4,384,512]{2,0,1:T(4,128)(2,1)} %copy.134), calls=%async_computation.1 | async-start | bytes 3145728 | tf_op jit(solution)/shard_map/all_to_all | solution.py:216
  142.7 62.6 %all-reduce.2.cloned.1.call-start = ((), (), s32[]{:S(2)}) async-start(), calls=%async_computation.4 | async-start | bytes 2170880 | tf_op jit(solution)/shard_map/psum | solution.py:48
  165.4 2.5 copy-start.8
  180.3 26.7 %copy-start.25 = (f32[256]{0:T(256)S(1)}, f32[256]{0:T(256)}, u32[]{:S(2)}) copy-start(f32[256]{0:T(256)} %copy-done.24) | copy-start | bytes 3076
  180.3 26.7 %copy-start.27 = (f32[256]{0:T(256)S(1)}, f32[256]{0:T(256)}, u32[]{:S(2)}) copy-start(f32[256]{0:T(256)} %copy-done.26) | copy-start | bytes 3076
  180.3 26.7 %copy-start.29 = (f32[256]{0:T(256)S(1)}, f32[256]{0:T(256)}, u32[]{:S(2)}) copy-start(f32[256]{0:T(256)} %copy-done.28) | copy-start | bytes 3076
  180.3 26.7 %copy-start.31 = (f32[256]{0:T(256)S(1)}, f32[256]{0:T(256)}, u32[]{:S(2)}) copy-start(f32[256]{0:T(256)} %copy-done.30) | copy-start | bytes 3076
  180.3 105.4 %all-to-all-start = ((bf16[4,384,512]{2,0,1:T(4,128)(2,1)}), bf16[4,384,512]{2,0,1:T(4,128)(2,1)}, u32[]{:S(2)}, u32[]{:S(2)}) async-start(bf16[4,384,512]{2,0,1:T(4,128)(2,1)} %copy.132), calls=%async_computation | async-start | bytes 3145728 | tf_op jit(solution)/shard_map/all_to_all | solution.py:215
  207.0 1.9 copy-start.9
  208.9 0.7 copy-start.16
  208.9 0.7 copy-start.18
  212.5 1.2 slice-start.1
  285.7 27.9 %all-to-all-start.2 = ((bf16[4,256,512]{2,0,1:T(4,128)(2,1)}), bf16[4,256,512]{2,0,1:T(4,128)(2,1)}, u32[]{:S(2)}, u32[]{:S(2)}) async-start(bf16[4,256,512]{2,0,1:T(4,128)(2,1)} %get-tuple-element.198), calls=%async_computation.2 | async-start | bytes 2097152 | tf_op jit(solution)/shard_map/all_to_all | solution.py:217
  302.4 6.0 %copy-start.11 = (f32[16384]{0:T(1024)S(1)}, f32[16384]{0:T(1024)}, u32[]{:S(2)}) copy-start(f32[16384]{0:T(1024)} %param.30) | copy-start | bytes 196612
  307.6 1.9 copy-start
  307.6 2.8 copy-start.1
  310.5 3.2 copy-start.3
  315.8 1.9 copy-start.5
  (2 other events, 1.4 us)
Sparse Core Ops, SparseCore 0:
  100.9 52.5 all-gather.3
  156.2 49.0 all-reduce.1
where the time goes:
time: 331 us; the launch traced here: 326 us
  local copies, waits for them, and re-layouts  99 us (30%)
  other arithmetic  59.6 us (18%)
  matrix products  50.9 us (15%)
  waiting for transfers between devices  50.8 us (15%)
  starting transfers between devices  40.4 us (12%)
  between operations  14.8 us (4%)
  blocking collectives  10.3 us (3%)
    dynamic_update_slice x8, local copies, waits for them, and re-layouts, per_device(): lax.map(option_work, (option_start, option_x_conv, option_bc_conv[..., :N...  42.6 us
    dot_general x8, matrix products, scan_block(): within = jnp.einsum('hts,shp->thp', weights, values, precision=highest)  22.5 us
    psum x1, waiting for transfers between devices, spread(): return lax.psum(block, axis)  18.8 us
    unnamed x75, local copies, waits for them, and re-layouts  16.1 us
    another operation x31, other arithmetic  16.1 us
    ppermute x2, waiting for transfers between devices, swapped(): return lax.ppermute(block, axis, route)  13.7 us
    dot_general x8, matrix products, scan_block(): jnp.einsum('tn,hpn->thp', c_rows.astype(jnp.float32), carry_state, precis...  10.9 us
    all_gather x1, blocking collectives, prefix(): gathered = jax.tree.map(lambda a: lax.all_gather(a, axis), part)  10.3 us
  transfers between devices with their start and end apart: 9, of which 5 were waited for; matrix products, arithmetic and copies ran while one was open for 40% of the time, Pallas kernels for 0%

commit v1 on v0

v1 whole, which is shorter than its diff:
```python
import functools

import jax
import jax.numpy as jnp
from jax import lax
from jax.experimental import pallas as pl
from jax.experimental.pallas import tpu as pltpu
from jax.sharding import PartitionSpec as P

NS = 128
GROUPS = 8
CHUNK = 128
HALO = 16
EPSILON = 1e-05
MESH = pl.DeviceIdType.MESH
MIB = 1 << 20


def silu(v):
    return v / (1.0 + jnp.exp(-v))


def dot(a, b, dims=((1,), (0,)), precision=None):
    return lax.dot_general(
        a, b, (dims, ((), ())), precision=precision, preferred_element_type=jnp.float32
    )


def conv_window(window, taps, rows):
    total = window[HALO - 3 : HALO - 3 + rows] * taps[0:1]
    for k in range(1, 4):
        total = total + window[HALO - 3 + k : HALO - 3 + k + rows] * taps[k : k + 1]
    return silu(total)


def mixer_kernel(
    heads,
    px, pbc, pg, pst, ox, obc, og, ost, xk, bck, sb, lr, sg,
    packed,
    xpad, xpado, gp, go, rim, gat, states, dec, xs, ee, rows, bu, cu, part, mid, ybuf, ybufo,
    load_sem, rim_send, rim_recv, bc_send, bc_recv, st_send, st_recv, dec_send, dec_recv,
):
    c = lax.axis_index("ctx")
    h = lax.axis_index("head")
    seqs, tokens, channels = px.shape
    opts, olen = ox.shape[0], ox.shape[1]
    nh = heads
    pk, ok = tokens // CHUNK, olen // CHUNK
    pchunks, chunks = seqs * pk, seqs * pk + opts * ok
    cols = pbc.shape[2]
    base = (h // 4) * 4
    r = lax.rem(h, 4)
    near = base + (r + 1 - 2 * lax.rem(r, 2))
    far = base + lax.rem(r + 2, 4)
    far_slot = lax.rem(r + 2, 4)
    half_p = seqs // 2 * tokens
    half_o = opts // 2 * olen

    loads = [
        pltpu.make_async_copy(px, xpad.at[:, pl.ds(HALO, tokens), :], load_sem.at[0]),
        pltpu.make_async_copy(ox, xpado.at[:, pl.ds(HALO, olen), :], load_sem.at[1]),
        pltpu.make_async_copy(pg, gp, load_sem.at[2]),
        pltpu.make_async_copy(og, go, load_sem.at[3]),
    ]
    for load in loads:
        load.start()

    barrier = pltpu.get_barrier_semaphore()
    for d in range(1, 4):
        pl.semaphore_signal(barrier, 1, device_id=(lax.rem(c + d, 4), h), device_id_type=MESH)
        pl.semaphore_signal(
            barrier, 1, device_id=(c, base + lax.rem(r + d, 4)), device_id_type=MESH
        )

    loads[0].wait()
    pad = jnp.zeros((HALO - 3 * seqs, channels), jnp.float32)
    tails = [xpad[s, tokens : tokens + HALO, :].astype(jnp.float32)[HALO - 3 :] for s in range(seqs)]
    rim[c, :, 0:channels] = jnp.concatenate(tails + [pad], axis=0).astype(jnp.bfloat16)
    pad = jnp.zeros((HALO - 3 * seqs, cols), jnp.float32)
    tails = [pbc[s, tokens - HALO : tokens, :].astype(jnp.float32)[HALO - 3 :] for s in range(seqs)]
    tails = jnp.concatenate(tails + [pad], axis=0)
    rim[c, :, channels : channels + 128] = jnp.concatenate(
        [tails, jnp.zeros((HALO, 128 - cols), jnp.float32)], axis=1
    ).astype(jnp.bfloat16)

    pl.semaphore_wait(barrier, 6)

    def rim_copy(d):
        return pltpu.make_async_remote_copy(
            src_ref=rim.at[c], dst_ref=rim.at[c], send_sem=rim_send.at[d - 1],
            recv_sem=rim_recv.at[d - 1], device_id=(lax.rem(c + d, 4), h), device_id_type=MESH,
        )

    def rim_arrival(d):
        source = lax.rem(c + 4 - d, 4)
        return pltpu.make_async_remote_copy(
            src_ref=rim.at[source], dst_ref=rim.at[source], send_sem=rim_send.at[d - 1],
            recv_sem=rim_recv.at[d - 1], device_id=(lax.rem(c + d, 4), h), device_id_type=MESH,
        )

    for d in range(1, 4):
        rim_copy(d).start()

    bias, rate = sb[...], -jnp.exp(lr[...])
    raw = [pst[s, k * CHUNK : (k + 1) * CHUNK, :] for s in range(seqs) for k in range(pk)]
    raw += [ost[o, k * CHUNK : (k + 1) * CHUNK, :] for o in range(opts) for k in range(ok)]
    raw = jnp.concatenate(raw, axis=1) + jnp.concatenate([bias] * chunks, axis=1)
    size = jnp.maximum(raw, 0.0) + jnp.log1p(jnp.exp(-jnp.abs(raw)))
    move = size * jnp.concatenate([rate] * chunks, axis=1)
    across = lax.broadcasted_iota(jnp.int32, (CHUNK, CHUNK), 0)
    along = lax.broadcasted_iota(jnp.int32, (CHUNK, CHUNK), 1)
    lower = across >= along
    cumul = dot(lower.astype(jnp.float32), move, precision=lax.Precision.HIGHEST)
    middle, end = cumul[CHUNK // 2 - 1 : CHUNK // 2], cumul[CHUNK - 1 : CHUNK]
    filler = jnp.zeros((13, end.shape[1]), jnp.float32)
    wide = jnp.concatenate(
        [
            jnp.exp(middle - cumul) * size,
            jnp.exp(cumul - middle),
            jnp.exp(end),
            jnp.exp(end - middle),
            jnp.exp(middle),
            filler,
        ],
        axis=0,
    )
    wide_high = wide.astype(jnp.bfloat16)
    wide_low = (wide - wide_high.astype(jnp.float32)).astype(jnp.bfloat16)
    lanes = wide.shape[1]
    per_head = channels // 8
    spread_row = lax.broadcasted_iota(jnp.int32, (lanes, channels), 0)
    spread_head = lax.div(lax.broadcasted_iota(jnp.int32, (lanes, channels), 1), per_head)

    for d in range(1, 4):
        rim_arrival(d).wait_recv()
    behind = lax.rem(c + 3, 4)
    has_behind = (c > 0).astype(jnp.float32)
    before = rim[behind].astype(jnp.float32) * has_behind
    last = rim[3].astype(jnp.float32)
    zeros = jnp.zeros((HALO - 3, channels), jnp.float32)
    owner_tail = jnp.zeros((3, channels + 128), jnp.float32)
    for s in range(seqs):
        tail = before[3 * s : 3 * s + 3]
        xpad[s, 0:HALO, :] = jnp.concatenate([zeros, tail[:, 0:channels]], axis=0).astype(jnp.bfloat16)
        owner_tail = owner_tail + last[3 * s : 3 * s + 3] * (c == s).astype(jnp.float32)
    loads[1].wait()
    for o in range(opts):
        xpado[o, 0:HALO, :] = jnp.concatenate([zeros, owner_tail[:, 0:channels]], axis=0).astype(
            jnp.bfloat16
        )

    taps = bck[...].astype(jnp.float32)
    taps = jnp.concatenate([taps, taps], axis=1)
    zeros = jnp.zeros((HALO - 3, 2 * cols), jnp.float32)
    for a in range(seqs // 2):
        tail = [before[3 * s : 3 * s + 3, channels : channels + cols] for s in (a, a + seqs // 2)]
        body = [pbc[s].astype(jnp.float32) for s in (a, a + seqs // 2)]
        window = jnp.concatenate(
            [zeros, jnp.concatenate(tail, axis=1), jnp.concatenate(body, axis=1)],
            axis=0,
        )
        gat[r, a * tokens : (a + 1) * tokens, :] = conv_window(window, taps, tokens).astype(jnp.bfloat16)
    tail = owner_tail[:, channels : channels + cols]
    tail = jnp.concatenate([tail, tail], axis=1)
    for a in range(opts // 2):
        body = [obc[o].astype(jnp.float32) for o in (a, a + opts // 2)]
        window = jnp.concatenate([zeros, tail, jnp.concatenate(body, axis=1)], axis=0)
        gat[r, half_p + a * olen : half_p + (a + 1) * olen, :] = conv_window(
            window, taps, olen
        ).astype(jnp.bfloat16)

    spans = ((0, half_p), (half_p, half_o))

    def bc_copy(part_no, way, slot, target):
        start, size_ = spans[part_no]
        ref = gat.at[slot, pl.ds(start, size_), :]
        return pltpu.make_async_remote_copy(
            src_ref=ref, dst_ref=ref, send_sem=bc_send.at[part_no, way],
            recv_sem=bc_recv.at[part_no, way], device_id=(c, target), device_id_type=MESH,
        )

    for part_no in range(2):
        bc_copy(part_no, 1, r, far).start()
        bc_copy(part_no, 0, r, near).start()

    near_slot = near - base
    cross_slot = lax.rem(near_slot + 2, 4)

    xtaps = xk[...].astype(jnp.float32)

    def convolve(j, window):
        out = conv_window(window, xtaps, CHUNK).astype(jnp.bfloat16)
        pick = (spread_row == 8 * j + spread_head).astype(jnp.bfloat16)
        grown = dot(wide_high, pick) + dot(wide_low, pick)
        xs[j] = (out.astype(jnp.float32) * grown[0:CHUNK]).astype(jnp.bfloat16)
        ee[j] = grown[CHUNK : 2 * CHUNK]
        rows[j] = grown[2 * CHUNK : 2 * CHUNK + 8]
        return out

    def prefix_conv(i, carry):
        s, k = i // pk, pk - 1 - lax.rem(i, pk)
        at = pl.multiple_of(k * CHUNK, CHUNK)
        window = xpad[s, pl.ds(at, CHUNK + HALO), :].astype(jnp.float32)
        xpad[s, pl.ds(at + HALO, CHUNK), :] = convolve(s * pk + k, window)
        return carry

    def option_conv(i, carry):
        o, k = i // ok, ok - 1 - lax.rem(i, ok)
        at = pl.multiple_of(k * CHUNK, CHUNK)
        window = xpado[o, pl.ds(at, CHUNK + HALO), :].astype(jnp.float32)
        xpado[o, pl.ds(at + HALO, CHUNK), :] = convolve(pchunks + o * ok + k, window)
        return carry

    lax.fori_loop(0, pchunks, prefix_conv, 0)
    lax.fori_loop(0, opts * ok, option_conv, 0)

    for s in range(seqs):
        total = rows[s * pk, 0:1, :]
        for k in range(1, pk):
            total = total * rows[s * pk + k, 0:1, :]
        dec[c, s : s + 1, :] = total

    def dec_copy(d, slot):
        return pltpu.make_async_remote_copy(
            src_ref=dec.at[slot], dst_ref=dec.at[slot], send_sem=dec_send.at[d - 1],
            recv_sem=dec_recv.at[d - 1], device_id=(lax.rem(c + d, 4), h), device_id_type=MESH,
        )

    for d in range(1, 4):
        dec_copy(d, c).start()

    left = lax.broadcasted_iota(jnp.int32, (CHUNK, 128), 1) < 64

    def unfold(start, low, high):
        parts = [gat[i, pl.ds(start, CHUNK), :].astype(jnp.float32) for i in range(4)]
        turned = [pltpu.roll(p, 64, 1) for p in parts]
        bu[low] = jnp.where(left, parts[0], turned[1]).astype(jnp.bfloat16)
        bu[high] = jnp.where(left, turned[0], parts[1]).astype(jnp.bfloat16)
        cu[low] = jnp.where(left, parts[2], turned[3]).astype(jnp.bfloat16)
        cu[high] = jnp.where(left, turned[2], parts[3]).astype(jnp.bfloat16)

    def unfold_prefix(i, carry):
        a, k = i // pk, lax.rem(i, pk)
        start = pl.multiple_of(i * CHUNK, CHUNK)
        unfold(start, a * pk + k, (a + seqs // 2) * pk + k)
        return carry

    def unfold_option(i, carry):
        a, k = i // ok, lax.rem(i, ok)
        start = pl.multiple_of(half_p + i * CHUNK, CHUNK)
        unfold(start, pchunks + a * ok + k, pchunks + (a + opts // 2) * ok + k)
        return carry

    bc_copy(0, 1, far_slot, far).wait_recv()
    bc_copy(0, 2, far_slot, near).start()
    bc_copy(0, 0, near_slot, near).wait_recv()
    bc_copy(0, 2, cross_slot, near).wait_recv()
    lax.fori_loop(0, seqs // 2 * pk, unfold_prefix, 0)

    def state_copy(d, s, slot):
        ref = states.at[slot, s]
        return pltpu.make_async_remote_copy(
            src_ref=ref, dst_ref=ref, send_sem=st_send.at[d - 1, s],
            recv_sem=st_recv.at[d - 1, s], device_id=(lax.rem(c + d, 4), h), device_id_type=MESH,
        )

    def local_states(s, carry):
        state = jnp.zeros((NS, channels), jnp.float32)
        for k in range(pk):
            j = s * pk + k
            if k > 0:
                part[s * (pk - 1) + k - 1] = state
            grown = dot(bu[j], xs[j], ((0,), (0,)))
            state = rows[j, 0:1, :] * state + rows[j, 1:2, :] * grown
        states[c, s] = state.astype(jnp.bfloat16)
        for d in range(1, 4):
            state_copy(d, s, c).start()
        return carry

    lax.fori_loop(0, seqs, local_states, 0)

    bc_copy(1, 1, far_slot, far).wait_recv()
    bc_copy(1, 2, far_slot, near).start()
    bc_copy(1, 0, near_slot, near).wait_recv()
    bc_copy(1, 2, cross_slot, near).wait_recv()
    lax.fori_loop(0, opts // 2 * ok, unfold_option, 0)

    for d in range(1, 4):
        dec_copy(d, lax.rem(c + 4 - d, 4)).wait_recv()
        for s in range(seqs):
            state_copy(d, s, lax.rem(c + 4 - d, 4)).wait_recv()

    skip = sg[...]
    skip = dot(
        jnp.concatenate(
            [
                skip.astype(jnp.bfloat16).astype(jnp.float32),
                skip - skip.astype(jnp.bfloat16).astype(jnp.float32),
                jnp.zeros((6, 8), jnp.float32),
            ],
            axis=0,
        ),
        (
            lax.broadcasted_iota(jnp.int32, (8, channels), 0)
            == lax.div(lax.broadcasted_iota(jnp.int32, (8, channels), 1), per_head)
        ).astype(jnp.float32),
    )
    skip = skip[0:1] + skip[1:2]

    def output(j, state, x, gate):
        scores = dot(cu[j], bu[j], ((1,), (1,)))
        scores = jnp.where(lower, scores, 0.0).astype(jnp.bfloat16)
        entering = (state * rows[j, 2:3, :]).astype(jnp.bfloat16)
        y = dot(scores, xs[j]) + dot(cu[j], entering)
        y = ee[j] * y + skip * x.astype(jnp.float32)
        return y * silu(gate.astype(jnp.float32))

    final = jnp.zeros((NS, channels), jnp.float32)
    for i in range(4):
        final = final * dec[i, pl.ds(c, 1), :] + states[i, c].astype(jnp.float32)
    mid[...] = final

    def option_out(o, carry):
        for k in range(ok):
            j = pchunks + o * ok + k
            state = mid[...]
            if k > 0:
                state = rows[j - 1, 0:1, :] * state + rows[j - 1, 1:2, :] * dot(
                    bu[j - 1], xs[j - 1], ((0,), (0,))
                )
            at = k * CHUNK
            ybufo[o, at : at + CHUNK, :] = output(
                j, state, xpado[o, HALO + at : HALO + at + CHUNK, :], go[o, at : at + CHUNK, :]
            )
        return carry

    loads[2].wait()
    loads[3].wait()
    lax.fori_loop(0, opts, option_out, 0)

    def prefix_out(s, carry):
        entering = jnp.zeros((NS, channels), jnp.float32)
        for i in range(3):
            step = entering * dec[i, pl.ds(s, 1), :] + states[i, s].astype(jnp.float32)
            entering = jnp.where(i < c, step, entering)
        mid[...] = entering
        factor = None
        for k in range(pk):
            j = s * pk + k
            state = mid[...]
            if k > 0:
                state = part[s * (pk - 1) + k - 1] + state * factor
            at = k * CHUNK
            ybuf[s, at : at + CHUNK, :] = output(
                j, state, xpad[s, HALO + at : HALO + at + CHUNK, :], gp[s, at : at + CHUNK, :]
            )
            factor = rows[j, 0:1, :] if k == 0 else factor * rows[j, 0:1, :]
        return carry

    lax.fori_loop(0, seqs, prefix_out, 0)

    pr, orr = tokens // nh, olen // nh

    def pack(i, carry):
        at = pl.multiple_of(2 * pr * i, 8)
        both = [ybuf[s, pl.ds(at, 2 * pr), :] for s in range(seqs)]
        for k in range(2):
            mine = [b[k * pr : (k + 1) * pr] for b in both]
            at_o = pl.multiple_of((2 * i + k) * orr, 8)
            mine += [ybufo[o, pl.ds(at_o, orr), :] for o in range(opts)]
            packed[2 * i + k] = jnp.concatenate(mine, axis=0).astype(jnp.bfloat16)
        return carry

    lax.fori_loop(0, nh // 2, pack, 0)

    for d in range(1, 4):
        rim_copy(d).wait_send()
        dec_copy(d, c).wait_send()
        for s in range(seqs):
            state_copy(d, s, c).wait_send()
    for part_no in range(2):
        bc_copy(part_no, 0, r, near).wait_send()
        bc_copy(part_no, 1, r, far).wait_send()
        bc_copy(part_no, 2, far_slot, near).wait_send()


def swap_kernel(heads, src, dst, own_sem, send_sem, recv_sem):
    c = lax.axis_index("ctx")
    h = lax.axis_index("head")
    own = pltpu.make_async_copy(src.at[h], dst.at[h], own_sem)
    own.start()
    barrier = pltpu.get_barrier_semaphore()

    def greet(d, carry):
        pl.semaphore_signal(
            barrier, 1, device_id=(c, lax.rem(h + d, heads)), device_id_type=MESH
        )
        return carry

    lax.fori_loop(1, heads, greet, 0)
    pl.semaphore_wait(barrier, heads - 1)

    def copy(d, target, slot):
        return pltpu.make_async_remote_copy(
            src_ref=src.at[target], dst_ref=dst.at[slot], send_sem=send_sem.at[d],
            recv_sem=recv_sem.at[d], device_id=(c, target), device_id_type=MESH,
        )

    def send(d, carry):
        copy(d, lax.rem(h + d, heads), h).start()
        return carry

    def finish(d, carry):
        copy(d, lax.rem(h + d, heads), h).wait_send()
        copy(d, lax.rem(h + d, heads), lax.rem(h + heads - d, heads)).wait_recv()
        return carry

    lax.fori_loop(1, heads, send, 0)
    lax.fori_loop(1, heads, finish, 0)
    own.wait()


def norm_kernel(seqs, pr, opts, orr, length, values, gain, prefix_out, option_out):
    h = lax.axis_index("head")
    blocks = [values[i].astype(jnp.float32) for i in range(4)]
    width = blocks[0].shape[1]
    total = sum(jnp.sum(b * b, axis=1, keepdims=True) for b in blocks)
    scale = lax.rsqrt(total / (4 * width) + EPSILON)
    first = seqs * pr
    place = lax.broadcasted_iota(jnp.int32, (orr, 1), 0) + h * orr
    for i in range(4):
        out = blocks[i] * scale * gain[:, i * width : (i + 1) * width]
        for s in range(seqs):
            prefix_out[s, :, i * width : (i + 1) * width] = out[s * pr : (s + 1) * pr].astype(jnp.bfloat16)
        for o in range(opts):
            keep = (place < length[o]).astype(jnp.float32)
            mine = out[first + o * orr : first + (o + 1) * orr] * keep
            option_out[o, :, i * width : (i + 1) * width] = mine.astype(jnp.bfloat16)


def per_device(
    prefix_x,
    prefix_bc,
    prefix_gate,
    prefix_steps,
    x_kernel,
    bc_kernel,
    step_bias,
    log_rate,
    skip_gain,
    norm_gain,
    option_x,
    option_bc,
    option_gate,
    option_steps,
    option_len,
):
    nh = lax.axis_size("head")
    seqs, tokens, channels = prefix_x.shape
    opts, olen = option_x.shape[0], option_x.shape[1]
    chunks = seqs * (tokens // CHUNK) + opts * (olen // CHUNK)
    half_rows = seqs // 2 * tokens + opts // 2 * olen
    pr, orr = tokens // nh, olen // nh
    block = seqs * pr + opts * orr
    bf16, f32 = jnp.bfloat16, jnp.float32
    anywhere = pl.BlockSpec(memory_space=pl.ANY)
    vmem = pl.BlockSpec(memory_space=pltpu.VMEM)
    dma = pltpu.SemaphoreType.DMA

    packed = pl.pallas_call(
        functools.partial(mixer_kernel, nh),
        out_shape=jax.ShapeDtypeStruct((nh, block, channels), bf16),
        in_specs=[anywhere, vmem, anywhere, vmem, anywhere, vmem, anywhere, vmem] + [vmem] * 5,
        out_specs=vmem,
        scratch_shapes=[
            pltpu.VMEM((seqs, HALO + tokens, channels), bf16),
            pltpu.VMEM((opts, HALO + olen, channels), bf16),
            pltpu.VMEM((seqs, tokens, channels), bf16),
            pltpu.VMEM((opts, olen, channels), bf16),
            pltpu.VMEM((4, HALO, channels + 128), bf16),
            pltpu.VMEM((4, half_rows, 128), bf16),
            pltpu.VMEM((4, seqs, NS, channels), bf16),
            pltpu.VMEM((4, 8, channels), f32),
            pltpu.VMEM((chunks, CHUNK, channels), bf16),
            pltpu.VMEM((chunks, CHUNK, channels), f32),
            pltpu.VMEM((chunks, 8, channels), f32),
            pltpu.VMEM((chunks, CHUNK, NS), bf16),
            pltpu.VMEM((chunks, CHUNK, NS), bf16),
            pltpu.VMEM((seqs * (tokens // CHUNK - 1), NS, channels), f32),
            pltpu.VMEM((NS, channels), f32),
            pltpu.VMEM((seqs, tokens, channels), f32),
            pltpu.VMEM((opts, olen, channels), f32),
            dma((4,)),
            dma((3,)), dma((3,)),
            dma((2, 3)), dma((2, 3)),
            dma((3, seqs)), dma((3, seqs)),
            dma((3,)), dma((3,)),
        ],
        compiler_params=pltpu.CompilerParams(
            collective_id=0, has_side_effects=True, vmem_limit_bytes=56 * MIB
        ),
        name="mixer",
    )(
        prefix_x, prefix_bc, prefix_gate, prefix_steps,
        option_x, option_bc, option_gate, option_steps,
        x_kernel, bc_kernel,
        step_bias.reshape(1, -1), log_rate.reshape(1, -1), skip_gain.reshape(1, -1),
    )

    swapped = pl.pallas_call(
        functools.partial(swap_kernel, nh),
        out_shape=jax.ShapeDtypeStruct((nh, block, channels), bf16),
        in_specs=[anywhere],
        out_specs=anywhere,
        scratch_shapes=[dma, dma((nh,)), dma((nh,))],
        compiler_params=pltpu.CompilerParams(collective_id=1, has_side_effects=True),
        name="swap",
    )(packed)

    group = 4 * channels
    inner = nh * channels
    return pl.pallas_call(
        functools.partial(norm_kernel, seqs, pr, opts, orr),
        grid_spec=pltpu.PrefetchScalarGridSpec(
            num_scalar_prefetch=1,
            grid=(nh // 4,),
            in_specs=[
                pl.BlockSpec((4, block, channels), lambda g, n: (g, 0, 0)),
                pl.BlockSpec((1, group), lambda g, n: (0, g)),
            ],
            out_specs=[
                pl.BlockSpec((seqs, pr, group), lambda g, n: (0, 0, g)),
                pl.BlockSpec((opts, orr, group), lambda g, n: (0, 0, g)),
            ],
        ),
        out_shape=[
            jax.ShapeDtypeStruct((seqs, pr, inner), bf16),
            jax.ShapeDtypeStruct((opts, orr, inner), bf16),
        ],
        compiler_params=pltpu.CompilerParams(vmem_limit_bytes=32 * MIB),
        name="norm",
    )(option_len, swapped, norm_gain.reshape(1, -1))


def solution(mesh):
    in_specs = (
        P(None, "ctx", "head"),
        P(None, "ctx", "head"),
        P(None, "ctx", "head"),
        P(None, "ctx", "head"),
        P(None, "head"),
        P(None, "head"),
        P("head"),
        P("head"),
        P("head"),
        P(),
        P("ctx", None, "head"),
        P("ctx", None, "head"),
        P("ctx", None, "head"),
        P("ctx", None, "head"),
        P("ctx"),
    )
    out_specs = (P(None, ("ctx", "head"), None), P("ctx", "head", None))
    return jax.shard_map(
        per_device, mesh=mesh, in_specs=in_specs, out_specs=out_specs, check_vma=False
    )
```

time: 331 us -> 118 us (0.36); the launches traced: 326 us -> 118 us
  Pallas kernels: 0 us -> 106 us
  local copies, waits for them, and re-layouts: 99 us -> 11.4 us
  other arithmetic: 59.6 us -> 0 us
  matrix products: 50.9 us -> 0 us
  waiting for transfers between devices: 50.8 us -> 0 us
  starting transfers between devices: 40.4 us -> 0 us
  between operations: 14.8 us -> 0.69 us
  blocking collectives: 10.3 us -> 0 us
    pallas_call x0 -> x3, Pallas kernels: none -> 106 us  [the longest x1 53.4 us: per_device(): pl.pallas_call(functools.partial(mixer_kernel, nh), out_shape=jax.ShapeDt...]
    dot_general x29 -> x0, matrix products: 50.9 us -> none  [the longest x8 22.5 us: scan_block(): within = jnp.einsum('hts,shp->thp', weights, values, precision=highest)]
    dynamic_update_slice x16 -> x0, local copies, waits for them, and re-layouts: 47.4 us -> none  [the longest x8 42.6 us: per_device(): lax.map(option_work, (option_start, option_x_conv, option_bc_conv[..., :N...]
    all_to_all x4 -> x0, starting transfers between devices: 34 us -> none  [the longest x1 9.79 us: per_device(): lax.all_to_all(option_gate, 'head', split_axis=1, concat_axis=2, tiled=True)]
    convert_element_type x16 -> x0, other arithmetic: 22 us -> none  [the longest x4 8.38 us: causal_conv(): return jax.nn.silu(summed).astype(jnp.bfloat16)]
    psum x1 -> x0, waiting for transfers between devices: 18.8 us -> none  [spread(): return lax.psum(block, axis)]
    another operation x31 -> x0, other arithmetic: 16.1 us -> none
    ppermute x3 -> x0, waiting for transfers between devices: 14.1 us -> none  [the longest x2 13.7 us: swapped(): return lax.ppermute(block, axis, route)]
  transfers between devices with their start and end apart: 9 -> 0, of which waited for: 5 -> 0; matrix products, arithmetic and copies ran while one was open for 40% -> 0% of each run, Pallas kernels for 0% -> 0%
where the time goes in v1:
time: 118 us
  Pallas kernels  106 us (90%)
  local copies, waits for them, and re-layouts  11.4 us (10%)
    pallas_call x1, Pallas kernels, per_device(): pl.pallas_call(functools.partial(mixer_kernel, nh), out_shape=jax.ShapeDt...  53.4 us
    pallas_call x1, Pallas kernels, per_device(): pl.pallas_call(functools.partial(swap_kernel, nh), out_shape=jax.ShapeDty...  48.1 us
    unnamed x10, local copies, waits for them, and re-layouts  9.07 us
    pallas_call x1, Pallas kernels, per_device(): pl.pallas_call(functools.partial(norm_kernel, seqs, pr, opts, orr), grid_...  4.31 us

profile of v1, /device:TPU:1, one launch (start us, length us, event | category | flops | bytes accessed | tf_op | source)
XLA Modules:
  0.0 117.9 jit_solution(3058604211862486698)
XLA Ops:
  0.6 1.8 %copy.19.obc = bf16[4,256,64]{2,1,0:T(8,128)(2,1)} copy(bf16[4,256,64]{1,2,0:T(8,128)(2,1)} %param.26) | data formatting | bytes 262144 | tf_op args[11]
  2.4 1.9 %copy.17.pbc = bf16[4,384,64]{2,1,0:T(8,128)(2,1)} copy(bf16[4,384,64]{1,2,0:T(8,128)(2,1)} %param.16) | data formatting | bytes 393216 | tf_op args[1]
  4.3 1.8 %copy.20.ost = f32[4,256,8]{2,1,0:T(8,128)} copy(f32[4,256,8]{1,2,0:T(8,128)} %param.28) | data formatting | bytes 65536 | tf_op args[13]
  6.0 1.9 %copy.18.pst = f32[4,384,8]{2,1,0:T(8,128)} copy(f32[4,384,8]{1,2,0:T(8,128)} %param.18) | data formatting | bytes 98304 | tf_op args[3]
  8.0 53.4 %mixer.1.src = bf16[32,80,512]{2,1,0:T(8,128)(2,1)} custom-call(bf16[4,384,512]{2,1,0:T(8,128)(2,1)} %px.1, bf16[4,384,64]{2,1,0:T(8,128)(2,1)} %copy.17.pbc, bf16[4,384,512]{2,1,0:T(8,128)(2,1)} %pg.1, f32[4,384,8]{2,1,0:T(8,128)} %copy.18.pst, bf16[4,256,512]{2,1,0:T(8,128)(2,1)} %ox.1, bf16[4,256,64]{2,1,0:T(8,128)(2,1)} %copy.19.obc, ...), custom_call_target="tpu_custom_call" | custom-call | tf_op jit(solution)/shard_map/mixer/pallas_call | solution.py:470
  61.3 0.0 copy-start.1
  61.4 0.0 copy-start.2
  61.4 48.1 %swap.1.values = bf16[32,80,512]{2,1,0:T(8,128)(2,1)} custom-call(bf16[32,80,512]{2,1,0:T(8,128)(2,1)} %mixer.1.src), custom_call_target="tpu_custom_call" | custom-call | tf_op jit(solution)/shard_map/swap/pallas_call | solution.py:510
  109.5 0.0 copy-done.1
  109.5 0.0 copy-done.2
  109.5 0.0 copy-start
  109.5 1.7 %copy-done = bf16[32,80,512]{2,1,0:T(8,128)(2,1)S(1)} copy-done((bf16[32,80,512]{2,1,0:T(8,128)(2,1)S(1)}, bf16[32,80,512]{2,1,0:T(8,128)(2,1)}, u32[]{:S(2)}) %copy-start) | copy-done | bytes 2621464
  111.2 4.3 %norm.1 = (bf16[4,12,16384]{2,1,0:T(8,128)(2,1)S(1)}, bf16[4,8,16384]{2,1,0:T(8,128)(2,1)}) custom-call(s32[4]{0:T(128)S(1)} %copy-done.2, bf16[32,80,512]{2,1,0:T(8,128)(2,1)S(1)} %copy-done, f32[1,16384]{1,0:T(1,128)S(1)} %bitcast.4), custom_call_target="tpu_custom_call" | custom-call | tf_op jit(solution)/shard_map/norm/pallas_call | solution.py:522
  115.5 2.4 %copy.21 = bf16[4,12,16384]{2,0,1:T(4,128)(2,1)} copy(bf16[4,12,16384]{2,1,0:T(8,128)(2,1)S(1)} %get-tuple-element.2) | data formatting | bytes 3145728 | tf_op jit(solution)/shard_map/norm/pallas_call | solution.py:522
Async XLA Ops:
  61.3 48.1 %copy-start.1 = (f32[16384]{0:T(1024)S(1)}, f32[16384]{0:T(1024)}, u32[]{:S(2)}) copy-start(f32[16384]{0:T(1024)} %param.24) | copy-start | bytes 196612
  61.4 48.1 %copy-start.2 = (s32[4]{0:T(128)S(1)}, s32[4]{0:T(128)}, u32[]{:S(2)}) copy-start(s32[4]{0:T(128)} %length.1) | copy-start | bytes 52
  109.5 1.7 %copy-start = (bf16[32,80,512]{2,1,0:T(8,128)(2,1)S(1)}, bf16[32,80,512]{2,1,0:T(8,128)(2,1)}, u32[]{:S(2)}) copy-start(bf16[32,80,512]{2,1,0:T(8,128)(2,1)} %swap.1.values) | copy-start | bytes 7864324

commit v2 on v1

v2 whole, which is shorter than its diff:
```python
import functools

import jax
import jax.numpy as jnp
from jax import lax
from jax.experimental import pallas as pl
from jax.experimental.pallas import tpu as pltpu
from jax.sharding import PartitionSpec as P

NS = 128
GROUPS = 8
CHUNK = 128
HALO = 16
EPSILON = 1e-05
MESH = pl.DeviceIdType.MESH
MIB = 1 << 20


def silu(v):
    return v / (1.0 + jnp.exp(-v))


def dot(a, b, dims=((1,), (0,)), precision=None):
    return lax.dot_general(
        a, b, (dims, ((), ())), precision=precision, preferred_element_type=jnp.float32
    )


def conv_window(window, taps, rows):
    total = window[HALO - 3 : HALO - 3 + rows] * taps[0:1]
    for k in range(1, 4):
        total = total + window[HALO - 3 + k : HALO - 3 + k + rows] * taps[k : k + 1]
    return silu(total)


def mixer_kernel(
    heads,
    px, pbc, pg, pst, ox, obc, og, ost, xk, bck, sb, lr, sg,
    out_p, out_o,
    xpad, xpado, gp, go, rim, gat, states, dec, xs, ee, rows, bu, cu, scores, part, ybuf, ybufo,
    pack_p, pack_o,
    load_sem, own_sem, rim_send, rim_recv, bc_send, bc_recv, ow_send, ow_recv, st_send, st_recv,
    dec_send, dec_recv, swap_send, swap_recv,
):
    c = lax.axis_index("ctx")
    h = lax.axis_index("head")
    seqs, tokens, channels = px.shape
    opts, olen = ox.shape[0], ox.shape[1]
    nh = heads
    pk, ok = tokens // CHUNK, olen // CHUNK
    pchunks, chunks = seqs * pk, seqs * pk + opts * ok
    cols = pbc.shape[1]
    half = channels // 2
    base = (h // 4) * 4
    r = lax.rem(h, 4)
    near = base + (r + 1 - 2 * lax.rem(r, 2))
    far = base + lax.rem(r + 2, 4)
    far_slot = lax.rem(r + 2, 4)
    near_slot = near - base
    cross_slot = lax.rem(near_slot + 2, 4)
    tops = (seqs // 2 + opts // 2) * HALO
    long_p, long_o = tokens - HALO, olen - HALO
    start_o = tops + seqs // 2 * long_p
    spans = ((0, tops), (tops, seqs // 2 * long_p), (start_o, opts // 2 * long_o))

    loads = [
        pltpu.make_async_copy(px, xpad.at[:, pl.ds(HALO, tokens), :], load_sem.at[0]),
        pltpu.make_async_copy(ox, xpado.at[:, pl.ds(HALO, olen), :], load_sem.at[1]),
        pltpu.make_async_copy(pg, gp, load_sem.at[2]),
        pltpu.make_async_copy(og, go, load_sem.at[3]),
    ]
    for load in loads:
        load.start()

    def partner(i):
        if nh != 32:
            return lax.rem(h + i, nh), lax.rem(h + nh - i, nh)
        z, y, k = h // 8, lax.rem(h // 2, 4), lax.rem(h, 2)
        dk, m = lax.rem(i, 2), i // 2
        dz, dy = lax.rem(m, 4), lax.rem(m // 4 + m, 4)
        core = lax.rem(k + dk, 2)
        to = lax.rem(z + dz, 4) * 8 + lax.rem(y + dy, 4) * 2 + core
        source = lax.rem(z + 4 - dz, 4) * 8 + lax.rem(y + 4 - dy, 4) * 2 + core
        return to, source

    barrier = pltpu.get_barrier_semaphore()

    def greet(i, carry):
        pl.semaphore_signal(barrier, 1, device_id=(c, lax.rem(h + i, nh)), device_id_type=MESH)
        return carry

    for d in range(1, 4):
        pl.semaphore_signal(barrier, 1, device_id=(lax.rem(c + d, 4), h), device_id_type=MESH)
    lax.fori_loop(1, nh, greet, 0)

    taps = bck[...].astype(jnp.float32)
    taps = jnp.concatenate([taps, taps], axis=1)
    blank = jnp.zeros((HALO, 2 * cols), jnp.float32)

    def pair(ref, a, count):
        both = jnp.concatenate([ref[a], ref[a + count // 2]], axis=0)
        return jnp.transpose(both.astype(jnp.float32))

    heads_p, heads_o, ends = [], [], []
    for a in range(seqs // 2):
        body = pair(pbc, a, seqs)
        heads_p.append(body[0:HALO])
        ends.append(body[tokens - 3 : tokens])
        out = conv_window(body, taps, long_p)
        gat[r, tops + a * long_p : tops + (a + 1) * long_p, :] = out.astype(jnp.bfloat16)
    for a in range(opts // 2):
        body = pair(obc, a, opts)
        heads_o.append(body[0:HALO])
        out = conv_window(body, taps, long_o)
        gat[r, start_o + a * long_o : start_o + (a + 1) * long_o, :] = out.astype(jnp.bfloat16)

    loads[0].wait()
    pad = jnp.zeros((HALO - 3 * seqs, channels), jnp.float32)
    tails = [xpad[s, tokens : tokens + HALO, :].astype(jnp.float32)[HALO - 3 :] for s in range(seqs)]
    rim[c, :, 0:channels] = jnp.concatenate(tails + [pad], axis=0).astype(jnp.bfloat16)
    pad = jnp.zeros((HALO - 3 * len(ends), 2 * cols), jnp.float32)
    rim[c, :, channels : channels + 2 * cols] = jnp.concatenate(ends + [pad], axis=0).astype(
        jnp.bfloat16
    )

    pl.semaphore_wait(barrier, nh + 2)

    def ctx_copy(ref, send, recv, d):
        return pltpu.make_async_remote_copy(
            src_ref=ref, dst_ref=ref, send_sem=send, recv_sem=recv,
            device_id=(lax.rem(c + d, 4), h), device_id_type=MESH,
        )

    def rim_copy(d, slot):
        return ctx_copy(rim.at[slot], rim_send.at[d - 1], rim_recv.at[d - 1], d)

    def bc_copy(part_no, way, slot, target):
        start, count = spans[part_no]
        ref = gat.at[slot, pl.ds(start, count), :]
        return pltpu.make_async_remote_copy(
            src_ref=ref, dst_ref=ref, send_sem=bc_send.at[part_no, way],
            recv_sem=bc_recv.at[part_no, way], device_id=(c, target), device_id_type=MESH,
        )

    for d in range(1, 4):
        rim_copy(d, c).start()
    for part_no in (1, 2):
        bc_copy(part_no, 1, r, far).start()
        bc_copy(part_no, 0, r, near).start()

    bias, rate = sb[...], -jnp.exp(lr[...])
    raw = [pst[s, :, k * CHUNK : (k + 1) * CHUNK] for s in range(seqs) for k in range(pk)]
    raw += [ost[o, :, k * CHUNK : (k + 1) * CHUNK] for o in range(opts) for k in range(ok)]
    raw += [jnp.zeros((256 - 8 * chunks, CHUNK), jnp.float32)]
    raw = jnp.transpose(jnp.concatenate(raw, axis=0))
    raw = raw + jnp.concatenate([bias] * 32, axis=1)
    size = jnp.maximum(raw, 0.0) + jnp.log1p(jnp.exp(-jnp.abs(raw)))
    move = size * jnp.concatenate([rate] * 32, axis=1)
    across = lax.broadcasted_iota(jnp.int32, (CHUNK, CHUNK), 0)
    along = lax.broadcasted_iota(jnp.int32, (CHUNK, CHUNK), 1)
    lower = across >= along
    cumul = dot(lower.astype(jnp.float32), move, precision=lax.Precision.HIGHEST)
    middle, end = cumul[CHUNK // 2 - 1 : CHUNK // 2], cumul[CHUNK - 1 : CHUNK]
    filler = jnp.zeros((13, end.shape[1]), jnp.float32)
    wide = jnp.concatenate(
        [
            jnp.exp(middle - cumul) * size,
            jnp.exp(cumul - middle),
            jnp.exp(end),
            jnp.exp(end - middle),
            jnp.exp(middle),
            filler,
        ],
        axis=0,
    )
    wide_high = wide.astype(jnp.bfloat16)
    wide_low = (wide - wide_high.astype(jnp.float32)).astype(jnp.bfloat16)
    lanes = wide.shape[1]
    per_head = channels // 8
    spread_row = lax.broadcasted_iota(jnp.int32, (lanes, channels), 0)
    spread_head = lax.div(lax.broadcasted_iota(jnp.int32, (lanes, channels), 1), per_head)

    xtaps = xk[...].astype(jnp.float32)

    def convolve(j, window):
        out = conv_window(window, xtaps, CHUNK).astype(jnp.bfloat16)
        pick = (spread_row == 8 * j + spread_head).astype(jnp.bfloat16)
        grown = dot(wide_high, pick) + dot(wide_low, pick)
        xs[j] = (out.astype(jnp.float32) * grown[0:CHUNK]).astype(jnp.bfloat16)
        ee[j] = grown[CHUNK : 2 * CHUNK]
        rows[j] = grown[2 * CHUNK : 2 * CHUNK + 8]
        return out

    def prefix_conv(s, k):
        at = k * CHUNK if isinstance(k, int) else pl.multiple_of(k * CHUNK, CHUNK)
        window = xpad[s, pl.ds(at, CHUNK + HALO), :].astype(jnp.float32)
        xpad[s, pl.ds(at + HALO, CHUNK), :] = convolve(s * pk + k, window)

    def option_conv(i, carry):
        o, k = i // ok, ok - 1 - lax.rem(i, ok)
        at = pl.multiple_of(k * CHUNK, CHUNK)
        window = xpado[o, pl.ds(at, CHUNK + HALO), :].astype(jnp.float32)
        xpado[o, pl.ds(at + HALO, CHUNK), :] = convolve(pchunks + o * ok + k, window)
        return carry

    def later_chunks(i, carry):
        prefix_conv(i // (pk - 1), pk - 1 - lax.rem(i, pk - 1))
        return carry

    def first_chunks(s, carry):
        prefix_conv(s, 0)
        return carry

    for d in range(1, 4):
        rim_copy(d, lax.rem(c + 4 - d, 4)).wait_recv()
    before = rim[lax.rem(c + 3, 4)].astype(jnp.float32) * (c > 0).astype(jnp.float32)
    last = rim[3].astype(jnp.float32)
    zeros = jnp.zeros((HALO - 3, channels), jnp.float32)
    owner_tail = jnp.zeros((3, channels), jnp.float32)
    owner_bc = jnp.zeros((3, cols), jnp.float32)
    for s in range(seqs):
        mine = (c == s).astype(jnp.float32)
        tail = before[3 * s : 3 * s + 3, 0:channels]
        xpad[s, 0:HALO, :] = jnp.concatenate([zeros, tail], axis=0).astype(jnp.bfloat16)
        owner_tail = owner_tail + last[3 * s : 3 * s + 3, 0:channels] * mine
        a, side = s % (seqs // 2), channels + cols * (s // (seqs // 2))
        owner_bc = owner_bc + last[3 * a : 3 * a + 3, side : side + cols] * mine
    loads[1].wait()
    for o in range(opts):
        xpado[o, 0:HALO, :] = jnp.concatenate([zeros, owner_tail], axis=0).astype(jnp.bfloat16)
    zeros = jnp.zeros((HALO - 3, 2 * cols), jnp.float32)
    for a in range(seqs // 2):
        tail = before[3 * a : 3 * a + 3, channels : channels + 2 * cols]
        window = jnp.concatenate([zeros, tail, heads_p[a]], axis=0)
        gat[r, a * HALO : (a + 1) * HALO, :] = conv_window(window, taps, HALO).astype(jnp.bfloat16)
    tail = jnp.concatenate([owner_bc, owner_bc], axis=1)
    for a in range(opts // 2):
        at = (seqs // 2 + a) * HALO
        window = jnp.concatenate([zeros, tail, heads_o[a]], axis=0)
        gat[r, at : at + HALO, :] = conv_window(window, taps, HALO).astype(jnp.bfloat16)
    bc_copy(0, 1, r, far).start()
    bc_copy(0, 0, r, near).start()

    lax.fori_loop(0, seqs * (pk - 1), later_chunks, 0)

    for part_no in (1, 0):
        bc_copy(part_no, 1, far_slot, far).wait_recv()
        bc_copy(part_no, 2, far_slot, near).start()

    lax.fori_loop(0, seqs, first_chunks, 0)

    for s in range(seqs):
        total = rows[s * pk, 0:1, :]
        for k in range(1, pk):
            total = total * rows[s * pk + k, 0:1, :]
        dec[c, s : s + 1, :] = total

    def dec_copy(d, slot):
        return ctx_copy(dec.at[slot], dec_send.at[d - 1], dec_recv.at[d - 1], d)

    for d in range(1, 4):
        dec_copy(d, c).start()

    left = lax.broadcasted_iota(jnp.int32, (CHUNK, 128), 1) < 64

    def unfold(top, start, low, high):
        if top is None:
            parts = [gat[i, pl.ds(start, CHUNK), :].astype(jnp.float32) for i in range(4)]
        else:
            parts = [
                jnp.concatenate(
                    [gat[i, pl.ds(top, HALO), :], gat[i, pl.ds(start, CHUNK - HALO), :]], axis=0
                ).astype(jnp.float32)
                for i in range(4)
            ]
        turned = [pltpu.roll(p, 64, 1) for p in parts]
        bu[low] = jnp.where(left, parts[0], turned[1]).astype(jnp.bfloat16)
        bu[high] = jnp.where(left, turned[0], parts[1]).astype(jnp.bfloat16)
        cu[low] = jnp.where(left, parts[2], turned[3]).astype(jnp.bfloat16)
        cu[high] = jnp.where(left, turned[2], parts[3]).astype(jnp.bfloat16)
        for j in (low, high):
            raw_scores = dot(cu[j], bu[j], ((1,), (1,)))
            scores[j] = jnp.where(lower, raw_scores, 0.0).astype(jnp.bfloat16)

    def unfold_prefix(a, carry):
        for k in range(pk):
            top = None if k else pl.multiple_of(a * HALO, HALO)
            start = tops + a * long_p + max(k * CHUNK - HALO, 0)
            unfold(top, pl.multiple_of(start, HALO), a * pk + k, (a + seqs // 2) * pk + k)
        return carry

    def unfold_option(a, carry):
        for k in range(ok):
            top = None if k else pl.multiple_of((seqs // 2 + a) * HALO, HALO)
            start = start_o + a * long_o + max(k * CHUNK - HALO, 0)
            unfold(
                top, pl.multiple_of(start, HALO),
                pchunks + a * ok + k, pchunks + (a + opts // 2) * ok + k,
            )
        return carry

    for part_no in (1, 0):
        bc_copy(part_no, 0, near_slot, near).wait_recv()
        bc_copy(part_no, 2, cross_slot, near).wait_recv()
    lax.fori_loop(0, seqs // 2, unfold_prefix, 0)

    def owner_copy(d, side, s, slot):
        return ctx_copy(
            states.at[slot, side, s], ow_send.at[d - 1, side], ow_recv.at[d - 1, side], d
        )

    def state_copy(d, side, n, s, slot):
        return ctx_copy(
            states.at[slot, side, s], st_send.at[d - 1, side, n], st_recv.at[d - 1, side, n], d
        )

    for d in range(1, 5):
        s = lax.rem(c + d, 4)
        state = jnp.zeros((NS, channels), jnp.float32)
        for k in range(pk):
            j = s * pk + k
            if k > 0:
                part[s * (pk - 1) + k - 1] = state
            grown = dot(bu[j], xs[j], ((0,), (0,)))
            state = rows[j, 0:1, :] * state + rows[j, 1:2, :] * grown
        for side in range(2):
            states[c, side, s] = state[:, side * half : (side + 1) * half].astype(jnp.bfloat16)
            if d < 4:
                owner_copy(d, side, s, c).start()

    def each_later(side, act):
        for d in range(1, 4):

            @pl.when(c + d < 4)
            def _():
                for n in range(3):
                    act(state_copy(d, side, n, lax.rem(c + d + 1 + n, 4), c))

    for side in range(2):
        each_later(side, lambda copy: copy.start())

    bc_copy(2, 1, far_slot, far).wait_recv()
    bc_copy(2, 2, far_slot, near).start()
    lax.fori_loop(0, opts * ok, option_conv, 0)
    bc_copy(2, 0, near_slot, near).wait_recv()
    bc_copy(2, 2, cross_slot, near).wait_recv()
    lax.fori_loop(0, opts // 2, unfold_option, 0)

    skip = sg[...]
    skip = dot(
        jnp.concatenate(
            [
                skip.astype(jnp.bfloat16).astype(jnp.float32),
                skip - skip.astype(jnp.bfloat16).astype(jnp.float32),
                jnp.zeros((6, 8), jnp.float32),
            ],
            axis=0,
        ),
        (
            lax.broadcasted_iota(jnp.int32, (8, channels), 0)
            == lax.div(lax.broadcasted_iota(jnp.int32, (8, channels), 1), per_head)
        ).astype(jnp.float32),
    )
    skip = skip[0:1] + skip[1:2]

    def output(j, lo, state, x, gate):
        at = slice(lo, lo + half)
        entering = (state * rows[j, 2:3, at]).astype(jnp.bfloat16)
        y = dot(scores[j], xs[j, :, at]) + dot(cu[j], entering)
        y = ee[j, :, at] * y + skip[:, at] * x.astype(jnp.float32)
        return y * silu(gate.astype(jnp.float32))

    pr, orr = tokens // nh, olen // nh

    def swap_copy(kind, side, i, slot_from, slot_to):
        packed, out = ((pack_o, out_o), (pack_p, out_p))[kind]
        to, _ = partner(i)
        return pltpu.make_async_remote_copy(
            src_ref=packed.at[side, slot_from], dst_ref=out.at[side, slot_to],
            send_sem=swap_send.at[kind, side, i], recv_sem=swap_recv.at[kind, side, i],
            device_id=(c, to), device_id_type=MESH,
        )

    def own_copy(kind, side):
        packed, out = ((pack_o, out_o), (pack_p, out_p))[kind]
        return pltpu.make_async_copy(packed.at[side, h], out.at[side, h], own_sem.at[kind, side])

    def send_all(kind, side):
        def send(i, carry):
            to, _ = partner(i)
            swap_copy(kind, side, i, to, h).start()
            return carry

        own_copy(kind, side).start()
        lax.fori_loop(1, nh, send, 0)

    def finish(kind, side):
        def one(i, carry):
            to, source = partner(i)
            swap_copy(kind, side, i, to, h).wait_send()
            swap_copy(kind, side, i, source, source).wait_recv()
            return carry

        own_copy(kind, side).wait()
        lax.fori_loop(1, nh, one, 0)

    for d in range(1, 4):
        dec_copy(d, lax.rem(c + 4 - d, 4)).wait_recv()
    loads[2].wait()
    loads[3].wait()
    for side in range(2):
        lo = side * half
        at = slice(lo, lo + half)
        for d in range(1, 4):
            owner_copy(d, side, c, lax.rem(c + 4 - d, 4)).wait_recv()
        final = jnp.zeros((NS, half), jnp.float32)
        for i in range(4):
            final = final * dec[i, pl.ds(c, 1), at] + states[i, side, c].astype(jnp.float32)

        def option_out(o, carry, side=side, lo=lo, at=at, final=final):
            state = final
            for k in range(ok):
                j = pchunks + o * ok + k
                if k > 0:
                    grown = dot(bu[j - 1], xs[j - 1, :, at], ((0,), (0,)))
                    state = rows[j - 1, 0:1, at] * state + rows[j - 1, 1:2, at] * grown
                p = k * CHUNK
                m = output(
                    j, lo, state, xpado[o, HALO + p : HALO + p + CHUNK, at], go[o, p : p + CHUNK, at]
                )
                some = CHUNK // orr
                ybufo[k * some : (k + 1) * some, pl.ds(pl.multiple_of(o * orr, 8), orr), :] = (
                    m.reshape(some, orr, half)
                )
            return carry

        lax.fori_loop(0, opts, option_out, 0)
        for i in range(nh):
            pack_o[side, i] = ybufo[i].astype(jnp.bfloat16)
        send_all(0, side)

    for side in range(2):
        lo = side * half
        at = slice(lo, lo + half)
        for d in range(1, 4):

            @pl.when(c >= d)
            def _():
                for n in range(3):
                    s = lax.rem(c + 1 + n, 4)
                    state_copy(d, side, n, s, lax.rem(c + 4 - d, 4)).wait_recv()

        def prefix_out(s, carry, side=side, lo=lo, at=at):
            state = jnp.zeros((NS, half), jnp.float32)
            for i in range(3):
                step = state * dec[i, pl.ds(s, 1), at] + states[i, side, s].astype(jnp.float32)
                state = jnp.where(i < c, step, state)
            factor = jnp.ones((1, half), jnp.float32)
            for k in range(pk):
                j = s * pk + k
                now = state if k == 0 else part[s * (pk - 1) + k - 1, :, at] + state * factor
                p = k * CHUNK
                m = output(
                    j, lo, now, xpad[s, HALO + p : HALO + p + CHUNK, at], gp[s, p : p + CHUNK, at]
                )
                for n in range(half // 128):
                    ybuf[n, pl.ds(seqs * p + s, CHUNK, seqs), :] = m[:, n * 128 : (n + 1) * 128]
                factor = factor * rows[j, 0:1, at]
            return carry

        lax.fori_loop(0, seqs, prefix_out, 0)

        def pack(i, carry, side=side):
            start = pl.multiple_of(i * seqs * pr, 16)
            for n in range(half // 128):
                pack_p[side, i, :, n * 128 : (n + 1) * 128] = ybuf[
                    n, pl.ds(start, seqs * pr), :
                ].astype(jnp.bfloat16)
            return carry

        lax.fori_loop(0, nh, pack, 0)
        send_all(1, side)

    for d in range(1, 4):
        rim_copy(d, c).wait_send()
        dec_copy(d, c).wait_send()
        for side in range(2):
            owner_copy(d, side, lax.rem(c + d, 4), c).wait_send()
    for side in range(2):
        each_later(side, lambda copy: copy.wait_send())
    for part_no in range(3):
        bc_copy(part_no, 0, r, near).wait_send()
        bc_copy(part_no, 1, r, far).wait_send()
        bc_copy(part_no, 2, far_slot, near).wait_send()
    for kind in range(2):
        for side in range(2):
            finish(kind, side)


def norm_kernel(seqs, pr, opts, orr, length, values_p, values_o, gain, prefix_out, option_out):
    h = lax.axis_index("head")
    half = values_p.shape[3]
    place = lax.broadcasted_iota(jnp.int32, (orr, 1), 0) + h * orr

    def scaled(values):
        blocks = [values[side, i].astype(jnp.float32) for i in range(4) for side in range(2)]
        total = sum(jnp.sum(b * b, axis=1, keepdims=True) for b in blocks)
        scale = lax.rsqrt(total / (8 * half) + EPSILON)
        return [b * scale * gain[:, n * half : (n + 1) * half] for n, b in enumerate(blocks)]

    for n, out in enumerate(scaled(values_p)):
        at = slice(n * half, (n + 1) * half)
        for i in range(pr):
            prefix_out[i, :, at] = out[i * seqs : (i + 1) * seqs].astype(jnp.bfloat16)
    keeps = [(place < length[o]).astype(jnp.float32) for o in range(opts)]
    for n, out in enumerate(scaled(values_o)):
        at = slice(n * half, (n + 1) * half)
        for o in range(opts):
            mine = out[o * orr : (o + 1) * orr] * keeps[o]
            option_out[o, :, at] = mine.astype(jnp.bfloat16)


def per_device(
    prefix_x,
    prefix_bc,
    prefix_gate,
    prefix_steps,
    x_kernel,
    bc_kernel,
    step_bias,
    log_rate,
    skip_gain,
    norm_gain,
    option_x,
    option_bc,
    option_gate,
    option_steps,
    option_len,
):
    nh = lax.axis_size("head")
    seqs, tokens, channels = prefix_x.shape
    opts, olen = option_x.shape[0], option_x.shape[1]
    chunks = seqs * (tokens // CHUNK) + opts * (olen // CHUNK)
    half_rows = seqs // 2 * tokens + opts // 2 * olen
    half = channels // 2
    pr, orr = tokens // nh, olen // nh
    bf16, f32 = jnp.bfloat16, jnp.float32
    anywhere = pl.BlockSpec(memory_space=pl.ANY)
    vmem = pl.BlockSpec(memory_space=pltpu.VMEM)
    dma = pltpu.SemaphoreType.DMA
    flip = functools.partial(jnp.swapaxes, axis1=1, axis2=2)

    swapped_p, swapped_o = pl.pallas_call(
        functools.partial(mixer_kernel, nh),
        out_shape=[
            jax.ShapeDtypeStruct((2, nh, seqs * pr, half), bf16),
            jax.ShapeDtypeStruct((2, nh, opts * orr, half), bf16),
        ],
        in_specs=[anywhere, vmem, anywhere, vmem, anywhere, vmem, anywhere, vmem] + [vmem] * 5,
        out_specs=[vmem, vmem],
        scratch_shapes=[
            pltpu.VMEM((seqs, HALO + tokens, channels), bf16),
            pltpu.VMEM((opts, HALO + olen, channels), bf16),
            pltpu.VMEM((seqs, tokens, channels), bf16),
            pltpu.VMEM((opts, olen, channels), bf16),
            pltpu.VMEM((4, HALO, channels + 128), bf16),
            pltpu.VMEM((4, half_rows, 128), bf16),
            pltpu.VMEM((4, 2, seqs, NS, half), bf16),
            pltpu.VMEM((4, 8, channels), f32),
            pltpu.VMEM((chunks, CHUNK, channels), bf16),
            pltpu.VMEM((chunks, CHUNK, channels), f32),
            pltpu.VMEM((chunks, 8, channels), f32),
            pltpu.VMEM((chunks, CHUNK, NS), bf16),
            pltpu.VMEM((chunks, CHUNK, NS), bf16),
            pltpu.VMEM((chunks, CHUNK, CHUNK), bf16),
            pltpu.VMEM((seqs * (tokens // CHUNK - 1), NS, channels), f32),
            pltpu.VMEM((half // 128, seqs * tokens, 128), f32),
            pltpu.VMEM((nh, opts * orr, half), f32),
            pltpu.VMEM((2, nh, seqs * pr, half), bf16),
            pltpu.VMEM((2, nh, opts * orr, half), bf16),
            dma((4,)),
            dma((2, 2)),
            dma((3,)), dma((3,)),
            dma((3, 3)), dma((3, 3)),
            dma((3, 2)), dma((3, 2)),
            dma((3, 2, 3)), dma((3, 2, 3)),
            dma((3,)), dma((3,)),
            dma((2, 2, nh)), dma((2, 2, nh)),
        ],
        compiler_params=pltpu.CompilerParams(
            collective_id=0, has_side_effects=True, vmem_limit_bytes=56 * MIB
        ),
        name="mixer",
    )(
        prefix_x, flip(prefix_bc), prefix_gate, flip(prefix_steps),
        option_x, flip(option_bc), option_gate, flip(option_steps),
        x_kernel, bc_kernel,
        step_bias.reshape(1, -1), log_rate.reshape(1, -1), skip_gain.reshape(1, -1),
    )

    group = 4 * channels
    inner = nh * channels
    prefix_out, option_out = pl.pallas_call(
        functools.partial(norm_kernel, seqs, pr, opts, orr),
        grid_spec=pltpu.PrefetchScalarGridSpec(
            num_scalar_prefetch=1,
            grid=(nh // 4,),
            in_specs=[
                pl.BlockSpec((2, 4, seqs * pr, half), lambda g, n: (0, g, 0, 0)),
                pl.BlockSpec((2, 4, opts * orr, half), lambda g, n: (0, g, 0, 0)),
                pl.BlockSpec((1, group), lambda g, n: (0, g)),
            ],
            out_specs=[
                pl.BlockSpec((pr, seqs, group), lambda g, n: (0, 0, g)),
                pl.BlockSpec((opts, orr, group), lambda g, n: (0, 0, g)),
            ],
        ),
        out_shape=[
            jax.ShapeDtypeStruct((pr, seqs, inner), bf16),
            jax.ShapeDtypeStruct((opts, orr, inner), bf16),
        ],
        compiler_params=pltpu.CompilerParams(vmem_limit_bytes=32 * MIB),
        name="norm",
    )(option_len, swapped_p, swapped_o, norm_gain.reshape(1, -1))
    return jnp.swapaxes(prefix_out, 0, 1), option_out


def solution(mesh):
    in_specs = (
        P(None, "ctx", "head"),
        P(None, "ctx", "head"),
        P(None, "ctx", "head"),
        P(None, "ctx", "head"),
        P(None, "head"),
        P(None, "head"),
        P("head"),
        P("head"),
        P("head"),
        P(),
        P("ctx", None, "head"),
        P("ctx", None, "head"),
        P("ctx", None, "head"),
        P("ctx", None, "head"),
        P("ctx"),
    )
    out_specs = (P(None, ("ctx", "head"), None), P("ctx", "head", None))
    return jax.shard_map(
        per_device, mesh=mesh, in_specs=in_specs, out_specs=out_specs, check_vma=False
    )
```

time: 118 us -> 73.9 us (0.63)
  Pallas kernels: 106 us -> 70.1 us
  local copies, waits for them, and re-layouts: 11.4 us -> 2.63 us
    pallas_call x2 -> x1, Pallas kernels: 101 us -> 65.4 us  [per_device(): pl.pallas_call(functools.partial(mixer_kernel, nh), out_shape=[jax.ShapeD...]
    unnamed x10 -> x8, local copies, waits for them, and re-layouts: 9.07 us -> 2.63 us
    pallas_call x1 -> x0, local copies, waits for them, and re-layouts: 2.36 us -> none  [per_device(): pl.pallas_call(functools.partial(norm_kernel, seqs, pr, opts, orr), grid_...]
where the time goes in v2:
time: 73.9 us; the launch traced here: 73.4 us
  Pallas kernels  70.1 us (95%)
  local copies, waits for them, and re-layouts  2.63 us (4%)
    pallas_call x1, Pallas kernels, per_device(): pl.pallas_call(functools.partial(mixer_kernel, nh), out_shape=[jax.ShapeD...  65.4 us
    pallas_call x1, Pallas kernels, per_device(): pl.pallas_call(functools.partial(norm_kernel, seqs, pr, opts, orr), grid_...  4.66 us
    unnamed x8, local copies, waits for them, and re-layouts  2.63 us

profile of v2, /device:TPU:1, one launch (start us, length us, event | category | flops | bytes accessed | tf_op | source)
XLA Modules:
  0.0 73.4 jit_solution(16376190066695896348)
XLA Ops:
  0.6 0.0 copy-start.2
  0.6 0.0 copy-start.3
  0.7 65.4 %mixer.1 = (bf16[2,32,48,256]{3,2,1,0:T(8,128)(2,1)}, bf16[2,32,32,256]{3,2,1,0:T(8,128)(2,1)}) custom-call(bf16[4,384,512]{2,1,0:T(8,128)(2,1)} %px.1, bf16[4,64,384]{2,1,0:T(8,128)(2,1)} %bitcast.10, bf16[4,384,512]{2,1,0:T(8,128)(2,1)} %pg.1, f32[4,8,384]{2,1,0:T(8,128)} %bitcast.12, bf16[4,256,512]{2,1,0:T(8,128)(2,1)} %ox.1, ...), custom_call_target="tpu_custom_call" | custom-call | tf_op jit(solution)/shard_map/mixer/pallas_call | solution.py:553
  66.1 0.0 copy-done.2
  66.1 0.0 copy-done.3
  66.1 0.0 copy-start
  66.1 1.4 %copy-done = bf16[2,32,48,256]{3,2,1,0:T(8,128)(2,1)S(1)} copy-done((bf16[2,32,48,256]{3,2,1,0:T(8,128)(2,1)S(1)}, bf16[2,32,48,256]{3,2,1,0:T(8,128)(2,1)}, u32[]{:S(2)}) %copy-start) | copy-done | bytes 1572888
  67.5 0.0 copy-start.1
  67.5 1.2 %copy-done.1 = bf16[2,32,32,256]{3,2,1,0:T(8,128)(2,1)S(1)} copy-done((bf16[2,32,32,256]{3,2,1,0:T(8,128)(2,1)S(1)}, bf16[2,32,32,256]{3,2,1,0:T(8,128)(2,1)}, u32[]{:S(2)}) %copy-start.1) | copy-done | bytes 1048600
  68.7 4.7 %norm.1 = (bf16[12,4,16384]{2,1,0:T(4,128)(2,1)}, bf16[4,8,16384]{2,1,0:T(8,128)(2,1)}) custom-call(s32[4]{0:T(128)S(1)} %copy-done.3, bf16[2,32,48,256]{3,2,1,0:T(8,128)(2,1)S(1)} %copy-done, bf16[2,32,32,256]{3,2,1,0:T(8,128)(2,1)S(1)} %copy-done.1, f32[1,16384]{1,0:T(1,128)S(1)} %bitcast.9), custom_call_target="tpu_custom_call" | custom-call | tf_op jit(solution)/shard_map/norm/pallas_call | solution.py:603
Async XLA Ops:
  0.6 65.5 %copy-start.2 = (f32[16384]{0:T(1024)S(1)}, f32[16384]{0:T(1024)}, u32[]{:S(2)}) copy-start(f32[16384]{0:T(1024)} %param.24) | copy-start | bytes 196612
  0.6 65.5 %copy-start.3 = (s32[4]{0:T(128)S(1)}, s32[4]{0:T(128)}, u32[]{:S(2)}) copy-start(s32[4]{0:T(128)} %length.1) | copy-start | bytes 52
  66.1 1.4 %copy-start = (bf16[2,32,48,256]{3,2,1,0:T(8,128)(2,1)S(1)}, bf16[2,32,48,256]{3,2,1,0:T(8,128)(2,1)}, u32[]{:S(2)}) copy-start(bf16[2,32,48,256]{3,2,1,0:T(8,128)(2,1)} %get-tuple-element.6.values_p) | copy-start | bytes 4718596
  67.5 1.2 %copy-start.1 = (bf16[2,32,32,256]{3,2,1,0:T(8,128)(2,1)S(1)}, bf16[2,32,32,256]{3,2,1,0:T(8,128)(2,1)}, u32[]{:S(2)}) copy-start(bf16[2,32,32,256]{3,2,1,0:T(8,128)(2,1)} %get-tuple-element.7.values_o) | copy-start | bytes 3145732

commit v3 on v2

--- a/solution.py
+++ b/solution.py
@@ -57,6 +57,7 @@
     far = base + lax.rem(r + 2, 4)
     far_slot = lax.rem(r + 2, 4)
     near_slot = near - base
+    cross = base + lax.rem(near_slot + 2, 4)
     cross_slot = lax.rem(near_slot + 2, 4)
     tops = (seqs // 2 + opts // 2) * HALO
     long_p, long_o = tokens - HALO, olen - HALO
@@ -74,14 +75,12 @@
 
     def partner(i):
         if nh != 32:
-            return lax.rem(h + i, nh), lax.rem(h + nh - i, nh)
+            return lax.rem(h + i, nh)
         z, y, k = h // 8, lax.rem(h // 2, 4), lax.rem(h, 2)
         dk, m = lax.rem(i, 2), i // 2
         dz, dy = lax.rem(m, 4), lax.rem(m // 4 + m, 4)
         core = lax.rem(k + dk, 2)
-        to = lax.rem(z + dz, 4) * 8 + lax.rem(y + dy, 4) * 2 + core
-        source = lax.rem(z + 4 - dz, 4) * 8 + lax.rem(y + 4 - dy, 4) * 2 + core
-        return to, source
+        return lax.rem(z + dz, 4) * 8 + lax.rem(y + dy, 4) * 2 + core
 
     barrier = pltpu.get_barrier_semaphore()
 
@@ -132,21 +131,20 @@
         )
 
     def rim_copy(d, slot):
-        return ctx_copy(rim.at[slot], rim_send.at[d - 1], rim_recv.at[d - 1], d)
+        return ctx_copy(rim.at[slot], rim_send.at[0], rim_recv.at[d - 1], d)
 
     def bc_copy(part_no, way, slot, target):
         start, count = spans[part_no]
         ref = gat.at[slot, pl.ds(start, count), :]
         return pltpu.make_async_remote_copy(
-            src_ref=ref, dst_ref=ref, send_sem=bc_send.at[part_no, way],
+            src_ref=ref, dst_ref=ref, send_sem=bc_send.at[0],
             recv_sem=bc_recv.at[part_no, way], device_id=(c, target), device_id_type=MESH,
         )
 
     for d in range(1, 4):
         rim_copy(d, c).start()
-    for part_no in (1, 2):
-        bc_copy(part_no, 1, r, far).start()
-        bc_copy(part_no, 0, r, near).start()
+    bc_copy(1, 1, r, far).start()
+    bc_copy(1, 0, r, near).start()
 
     bias, rate = sb[...], -jnp.exp(lr[...])
     raw = [pst[s, :, k * CHUNK : (k + 1) * CHUNK] for s in range(seqs) for k in range(pk)]
@@ -239,13 +237,15 @@
         window = jnp.concatenate([zeros, tail, heads_o[a]], axis=0)
         gat[r, at : at + HALO, :] = conv_window(window, taps, HALO).astype(jnp.bfloat16)
     bc_copy(0, 1, r, far).start()
+    bc_copy(0, 2, r, cross).start()
     bc_copy(0, 0, r, near).start()
+    bc_copy(2, 1, r, far).start()
+    bc_copy(2, 0, r, near).start()
 
     lax.fori_loop(0, seqs * (pk - 1), later_chunks, 0)
 
-    for part_no in (1, 0):
-        bc_copy(part_no, 1, far_slot, far).wait_recv()
-        bc_copy(part_no, 2, far_slot, near).start()
+    bc_copy(1, 1, far_slot, far).wait_recv()
+    bc_copy(1, 2, far_slot, near).start()
 
     lax.fori_loop(0, seqs, first_chunks, 0)
 
@@ -256,62 +256,74 @@
         dec[c, s : s + 1, :] = total
 
     def dec_copy(d, slot):
-        return ctx_copy(dec.at[slot], dec_send.at[d - 1], dec_recv.at[d - 1], d)
+        return ctx_copy(dec.at[slot], dec_send.at[0], dec_recv.at[d - 1], d)
 
     for d in range(1, 4):
         dec_copy(d, c).start()
 
     left = lax.broadcasted_iota(jnp.int32, (CHUNK, 128), 1) < 64
 
-    def unfold(top, start, low, high):
+    def unfold(to, first, top, start, low, high):
         if top is None:
-            parts = [gat[i, pl.ds(start, CHUNK), :].astype(jnp.float32) for i in range(4)]
+            parts = [gat[first + i, pl.ds(start, CHUNK), :].astype(jnp.float32) for i in range(2)]
         else:
             parts = [
                 jnp.concatenate(
-                    [gat[i, pl.ds(top, HALO), :], gat[i, pl.ds(start, CHUNK - HALO), :]], axis=0
+                    [
+                        gat[first + i, pl.ds(top, HALO), :],
+                        gat[first + i, pl.ds(start, CHUNK - HALO), :],
+                    ],
+                    axis=0,
                 ).astype(jnp.float32)
-                for i in range(4)
+                for i in range(2)
             ]
         turned = [pltpu.roll(p, 64, 1) for p in parts]
-        bu[low] = jnp.where(left, parts[0], turned[1]).astype(jnp.bfloat16)
-        bu[high] = jnp.where(left, turned[0], parts[1]).astype(jnp.bfloat16)
-        cu[low] = jnp.where(left, parts[2], turned[3]).astype(jnp.bfloat16)
-        cu[high] = jnp.where(left, turned[2], parts[3]).astype(jnp.bfloat16)
-        for j in (low, high):
-            raw_scores = dot(cu[j], bu[j], ((1,), (1,)))
-            scores[j] = jnp.where(lower, raw_scores, 0.0).astype(jnp.bfloat16)
-
-    def unfold_prefix(a, carry):
-        for k in range(pk):
-            top = None if k else pl.multiple_of(a * HALO, HALO)
-            start = tops + a * long_p + max(k * CHUNK - HALO, 0)
-            unfold(top, pl.multiple_of(start, HALO), a * pk + k, (a + seqs // 2) * pk + k)
+        to[low] = jnp.where(left, parts[0], turned[1]).astype(jnp.bfloat16)
+        to[high] = jnp.where(left, turned[0], parts[1]).astype(jnp.bfloat16)
+
+    def unfold_prefix(to, first):
+        def one(a, carry):
+            for k in range(pk):
+                top = None if k else pl.multiple_of(a * HALO, HALO)
+                start = tops + a * long_p + max(k * CHUNK - HALO, 0)
+                start = pl.multiple_of(start, HALO)
+                unfold(to, first, top, start, a * pk + k, (a + seqs // 2) * pk + k)
+            return carry
+
+        lax.fori_loop(0, seqs // 2, one, 0)
+
+    def unfold_option(to, first):
+        def one(a, carry):
+            for k in range(ok):
+                top = None if k else pl.multiple_of((seqs // 2 + a) * HALO, HALO)
+                start = start_o + a * long_o + max(k * CHUNK - HALO, 0)
+                start = pl.multiple_of(start, HALO)
+                low = pchunks + a * ok + k
+                unfold(to, first, top, start, low, low + opts // 2 * ok)
+            return carry
+
+        lax.fori_loop(0, opts // 2, one, 0)
+
+    def score(j, carry):
+        raw_scores = dot(cu[j], bu[j], ((1,), (1,)))
+        scores[j] = jnp.where(lower, raw_scores, 0.0).astype(jnp.bfloat16)
         return carry
 
-    def unfold_option(a, carry):
-        for k in range(ok):
-            top = None if k else pl.multiple_of((seqs // 2 + a) * HALO, HALO)
-            start = start_o + a * long_o + max(k * CHUNK - HALO, 0)
-            unfold(
-                top, pl.multiple_of(start, HALO),
-                pchunks + a * ok + k, pchunks + (a + opts // 2) * ok + k,
-            )
-        return carry
-
-    for part_no in (1, 0):
-        bc_copy(part_no, 0, near_slot, near).wait_recv()
-        bc_copy(part_no, 2, cross_slot, near).wait_recv()
-    lax.fori_loop(0, seqs // 2, unfold_prefix, 0)
+    bc_copy(0, 0, near_slot, near).wait_recv()
+    bc_copy(0, 1, far_slot, far).wait_recv()
+    bc_copy(0, 2, cross_slot, cross).wait_recv()
+    bc_copy(1, 0, near_slot, near).wait_recv()
+    bc_copy(1, 2, cross_slot, near).wait_recv()
+    unfold_prefix(bu, 0)
 
     def owner_copy(d, side, s, slot):
         return ctx_copy(
-            states.at[slot, side, s], ow_send.at[d - 1, side], ow_recv.at[d - 1, side], d
+            states.at[slot, side, s], ow_send.at[0], ow_recv.at[d - 1, side], d
         )
 
-    def state_copy(d, side, n, s, slot):
+    def state_copy(d, side, s, slot):
         return ctx_copy(
-            states.at[slot, side, s], st_send.at[d - 1, side, n], st_recv.at[d - 1, side, n], d
+            states.at[slot, side, s], st_send.at[d - 1], st_recv.at[d - 1, side], d
         )
 
     for d in range(1, 5):
@@ -328,23 +340,23 @@
             if d < 4:
                 owner_copy(d, side, s, c).start()
 
-    def each_later(side, act):
+    for side in range(2):
         for d in range(1, 4):
 
             @pl.when(c + d < 4)
             def _():
                 for n in range(3):
-                    act(state_copy(d, side, n, lax.rem(c + d + 1 + n, 4), c))
-
-    for side in range(2):
-        each_later(side, lambda copy: copy.start())
+                    state_copy(d, side, lax.rem(c + d + 1 + n, 4), c).start()
 
     bc_copy(2, 1, far_slot, far).wait_recv()
     bc_copy(2, 2, far_slot, near).start()
     lax.fori_loop(0, opts * ok, option_conv, 0)
     bc_copy(2, 0, near_slot, near).wait_recv()
     bc_copy(2, 2, cross_slot, near).wait_recv()
-    lax.fori_loop(0, opts // 2, unfold_option, 0)
+    unfold_option(bu, 0)
+    unfold_option(cu, 2)
+    unfold_prefix(cu, 2)
+    lax.fori_loop(0, chunks, score, 0)
 
     skip = sg[...]
     skip = dot(
@@ -372,12 +384,11 @@
 
     pr, orr = tokens // nh, olen // nh
 
-    def swap_copy(kind, side, i, slot_from, slot_to):
+    def swap_copy(kind, side, to):
         packed, out = ((pack_o, out_o), (pack_p, out_p))[kind]
-        to, _ = partner(i)
         return pltpu.make_async_remote_copy(
-            src_ref=packed.at[side, slot_from], dst_ref=out.at[side, slot_to],
-            send_sem=swap_send.at[kind, side, i], recv_sem=swap_recv.at[kind, side, i],
+            src_ref=packed.at[side, to], dst_ref=out.at[side, h],
+            send_sem=swap_send.at[kind, side], recv_sem=swap_recv.at[kind, side],
             device_id=(c, to), device_id_type=MESH,
         )
 
@@ -387,22 +398,23 @@
 
     def send_all(kind, side):
         def send(i, carry):
-            to, _ = partner(i)
-            swap_copy(kind, side, i, to, h).start()
+            swap_copy(kind, side, partner(i)).start()
             return carry
 
         own_copy(kind, side).start()
         lax.fori_loop(1, nh, send, 0)
 
     def finish(kind, side):
-        def one(i, carry):
-            to, source = partner(i)
-            swap_copy(kind, side, i, to, h).wait_send()
-            swap_copy(kind, side, i, source, source).wait_recv()
-            return carry
-
+        packed, out = ((pack_o, out_o), (pack_p, out_p))[kind]
+        others = pl.ds(0, nh - 1)
+        every = pltpu.make_async_remote_copy(
+            src_ref=packed.at[side, others], dst_ref=out.at[side, others],
+            send_sem=swap_send.at[kind, side], recv_sem=swap_recv.at[kind, side],
+            device_id=(c, near), device_id_type=MESH,
+        )
         own_copy(kind, side).wait()
-        lax.fori_loop(1, nh, one, 0)
+        every.wait_send()
+        every.wait_recv()
 
     for d in range(1, 4):
         dec_copy(d, lax.rem(c + 4 - d, 4)).wait_recv()
@@ -446,9 +458,8 @@
 
             @pl.when(c >= d)
             def _():
-                for n in range(3):
-                    s = lax.rem(c + 1 + n, 4)
-                    state_copy(d, side, n, s, lax.rem(c + 4 - d, 4)).wait_recv()
+                ref = states.at[lax.rem(c + 4 - d, 4), side, pl.ds(0, 3)]
+                ctx_copy(ref, st_send.at[d - 1], st_recv.at[d - 1, side], d).wait_recv()
 
         def prefix_out(s, carry, side=side, lo=lo, at=at):
             state = jnp.zeros((NS, half), jnp.float32)
@@ -481,43 +492,85 @@
         lax.fori_loop(0, nh, pack, 0)
         send_all(1, side)
 
+    ctx_copy(rim.at[pl.ds(0, 3)], rim_send.at[0], rim_recv.at[0], 1).wait_send()
+    ctx_copy(dec.at[pl.ds(0, 3)], dec_send.at[0], dec_recv.at[0], 1).wait_send()
+    some = states.at[0, :, pl.ds(0, 3)]
+    ctx_copy(some, ow_send.at[0], ow_recv.at[0, 0], 1).wait_send()
     for d in range(1, 4):
-        rim_copy(d, c).wait_send()
-        dec_copy(d, c).wait_send()
-        for side in range(2):
-            owner_copy(d, side, lax.rem(c + d, 4), c).wait_send()
-    for side in range(2):
-        each_later(side, lambda copy: copy.wait_send())
-    for part_no in range(3):
-        bc_copy(part_no, 0, r, near).wait_send()
-        bc_copy(part_no, 1, r, far).wait_send()
-        bc_copy(part_no, 2, far_slot, near).wait_send()
+
+        @pl.when(c + d < 4)
+        def _():
+            ctx_copy(some, st_send.at[d - 1], st_recv.at[d - 1, 0], 1).wait_send()
+
+    some = gat.at[pl.ds(0, 3)]
+    pltpu.make_async_remote_copy(
+        src_ref=some, dst_ref=some, send_sem=bc_send.at[0], recv_sem=bc_recv.at[0, 0],
+        device_id=(c, near), device_id_type=MESH,
+    ).wait_send()
     for kind in range(2):
         for side in range(2):
             finish(kind, side)
 
 
-def norm_kernel(seqs, pr, opts, orr, length, values_p, values_o, gain, prefix_out, option_out):
+def norm_kernel(
+    seqs, pr, opts, orr, length, values_p, values_o, gain, prefix_out, option_out,
+    buf_p, buf_o, res_p, res_o, sems, out_sems,
+):
     h = lax.axis_index("head")
     half = values_p.shape[3]
+    groups = values_p.shape[1] // 4
+    width = 8 * half
     place = lax.broadcasted_iota(jnp.int32, (orr, 1), 0) + h * orr
-
-    def scaled(values):
-        blocks = [values[side, i].astype(jnp.float32) for i in range(4) for side in range(2)]
-        total = sum(jnp.sum(b * b, axis=1, keepdims=True) for b in blocks)
-        scale = lax.rsqrt(total / (8 * half) + EPSILON)
-        return [b * scale * gain[:, n * half : (n + 1) * half] for n, b in enumerate(blocks)]
-
-    for n, out in enumerate(scaled(values_p)):
-        at = slice(n * half, (n + 1) * half)
-        for i in range(pr):
-            prefix_out[i, :, at] = out[i * seqs : (i + 1) * seqs].astype(jnp.bfloat16)
     keeps = [(place < length[o]).astype(jnp.float32) for o in range(opts)]
-    for n, out in enumerate(scaled(values_o)):
-        at = slice(n * half, (n + 1) * half)
-        for o in range(opts):
-            mine = out[o * orr : (o + 1) * orr] * keeps[o]
-            option_out[o, :, at] = mine.astype(jnp.bfloat16)
+
+    def fetch(group):
+        at = pl.ds(group * 4, 4)
+        return [
+            pltpu.make_async_copy(values.at[:, at], buf.at[:, at], sems.at[n, group])
+            for n, (values, buf) in enumerate(((values_p, buf_p), (values_o, buf_o)))
+        ]
+
+    def store(group):
+        at = pl.ds(group * width, width)
+        return [
+            pltpu.make_async_copy(res.at[:, :, at], out.at[:, :, at], out_sems.at[n, group])
+            for n, (res, out) in enumerate(((res_p, prefix_out), (res_o, option_out)))
+        ]
+
+    for group in range(groups):
+        for copy in fetch(group):
+            copy.start()
+
+    def scale(buf, group):
+        squares = None
+        for side in range(2):
+            for i in range(4):
+                block = buf[side, group * 4 + i].astype(jnp.float32)
+                squares = block * block if squares is None else squares + block * block
+        total = jnp.sum(squares, axis=1, keepdims=True)
+        return lax.rsqrt(total / (8 * half) + EPSILON)
+
+    for group in range(groups):
+        for copy in fetch(group):
+            copy.wait()
+        scale_p = scale(buf_p, group)
+        scale_o = scale(buf_o, group)
+        scale_o = jnp.concatenate(
+            [scale_o[o * orr : (o + 1) * orr] * keeps[o] for o in range(opts)], axis=0
+        )
+        for i in range(4):
+            for side in range(2):
+                lo = (group * 8 + i * 2 + side) * half
+                at = slice(lo, lo + half)
+                out = buf_p[side, group * 4 + i].astype(jnp.float32) * scale_p * gain[:, at]
+                res_p[:, :, at] = out.reshape(pr, seqs, half).astype(jnp.bfloat16)
+                out = buf_o[side, group * 4 + i].astype(jnp.float32) * scale_o * gain[:, at]
+                res_o[:, :, at] = out.reshape(opts, orr, half).astype(jnp.bfloat16)
+        for copy in store(group):
+            copy.start()
+    for group in range(groups):
+        for copy in store(group):
+            copy.wait()
 
 
 def per_device(
@@ -557,7 +610,7 @@
             jax.ShapeDtypeStruct((2, nh, opts * orr, half), bf16),
         ],
         in_specs=[anywhere, vmem, anywhere, vmem, anywhere, vmem, anywhere, vmem] + [vmem] * 5,
-        out_specs=[vmem, vmem],
+        out_specs=[anywhere, anywhere],
         scratch_shapes=[
             pltpu.VMEM((seqs, HALO + tokens, channels), bf16),
             pltpu.VMEM((opts, HALO + olen, channels), bf16),
@@ -580,15 +633,15 @@
             pltpu.VMEM((2, nh, opts * orr, half), bf16),
             dma((4,)),
             dma((2, 2)),
-            dma((3,)), dma((3,)),
-            dma((3, 3)), dma((3, 3)),
-            dma((3, 2)), dma((3, 2)),
-            dma((3, 2, 3)), dma((3, 2, 3)),
-            dma((3,)), dma((3,)),
-            dma((2, 2, nh)), dma((2, 2, nh)),
+            dma((1,)), dma((3,)),
+            dma((1,)), dma((3, 3)),
+            dma((1,)), dma((3, 2)),
+            dma((3,)), dma((3, 2)),
+            dma((1,)), dma((3,)),
+            dma((2, 2)), dma((2, 2)),
         ],
         compiler_params=pltpu.CompilerParams(
-            collective_id=0, has_side_effects=True, vmem_limit_bytes=56 * MIB
+            collective_id=0, has_side_effects=True, vmem_limit_bytes=54 * MIB
         ),
         name="mixer",
     )(
@@ -598,28 +651,24 @@
         step_bias.reshape(1, -1), log_rate.reshape(1, -1), skip_gain.reshape(1, -1),
     )
 
-    group = 4 * channels
     inner = nh * channels
     prefix_out, option_out = pl.pallas_call(
         functools.partial(norm_kernel, seqs, pr, opts, orr),
-        grid_spec=pltpu.PrefetchScalarGridSpec(
-            num_scalar_prefetch=1,
-            grid=(nh // 4,),
-            in_specs=[
-                pl.BlockSpec((2, 4, seqs * pr, half), lambda g, n: (0, g, 0, 0)),
-                pl.BlockSpec((2, 4, opts * orr, half), lambda g, n: (0, g, 0, 0)),
-                pl.BlockSpec((1, group), lambda g, n: (0, g)),
-            ],
-            out_specs=[
-                pl.BlockSpec((pr, seqs, group), lambda g, n: (0, 0, g)),
-                pl.BlockSpec((opts, orr, group), lambda g, n: (0, 0, g)),
-            ],
-        ),
+        in_specs=[pl.BlockSpec(memory_space=pltpu.SMEM), anywhere, anywhere, vmem],
+        out_specs=[anywhere, anywhere],
+        scratch_shapes=[
+            pltpu.VMEM((2, nh, seqs * pr, half), bf16),
+            pltpu.VMEM((2, nh, opts * orr, half), bf16),
+            pltpu.VMEM((pr, seqs, inner), bf16),
+            pltpu.VMEM((opts, orr, inner), bf16),
+            dma((2, nh // 4)),
+            dma((2, nh // 4)),
+        ],
         out_shape=[
             jax.ShapeDtypeStruct((pr, seqs, inner), bf16),
             jax.ShapeDtypeStruct((opts, orr, inner), bf16),
         ],
-        compiler_params=pltpu.CompilerParams(vmem_limit_bytes=32 * MIB),
+        compiler_params=pltpu.CompilerParams(vmem_limit_bytes=60 * MIB),
         name="norm",
     )(option_len, swapped_p, swapped_o, norm_gain.reshape(1, -1))
     return jnp.swapaxes(prefix_out, 0, 1), option_out

time: 73.9 us -> 67.5 us (0.913)
  Pallas kernels: 70.1 us -> 66.6 us
  local copies, waits for them, and re-layouts: 2.63 us -> 0 us
    pallas_call x1, Pallas kernels: 65.4 us -> 62.1 us  [per_device(): pl.pallas_call(functools.partial(mixer_kernel, nh), out_shape=[jax.ShapeD...]
    unnamed x8 -> x0, local copies, waits for them, and re-layouts: 2.63 us -> none
where the time goes in v3:
time: 67.5 us; the launch traced here: 67.3 us
  Pallas kernels  66.6 us (99%)
    pallas_call x1, Pallas kernels, per_device(): pl.pallas_call(functools.partial(mixer_kernel, nh), out_shape=[jax.ShapeD...  62.1 us
    pallas_call x1, Pallas kernels, per_device(): pl.pallas_call(functools.partial(norm_kernel, seqs, pr, opts, orr), in_sp...  4.52 us

profile of v3, /device:TPU:1, one launch (start us, length us, event | category | flops | bytes accessed | tf_op | source)
XLA Modules:
  0.0 67.3 jit_solution(10864633097698107998)
XLA Ops:
  0.6 62.1 %mixer.1 = (bf16[2,32,48,256]{3,2,1,0:T(8,128)(2,1)}, bf16[2,32,32,256]{3,2,1,0:T(8,128)(2,1)}) custom-call(bf16[4,384,512]{2,1,0:T(8,128)(2,1)} %px.1, bf16[4,64,384]{2,1,0:T(8,128)(2,1)} %bitcast.9, bf16[4,384,512]{2,1,0:T(8,128)(2,1)} %pg.1, f32[4,8,384]{2,1,0:T(8,128)} %bitcast.12, bf16[4,256,512]{2,1,0:T(8,128)(2,1)} %ox.1, ...), custom_call_target="tpu_custom_call" | custom-call | tf_op jit(solution)/shard_map/mixer/pallas_call | solution.py:606
  62.8 4.5 %norm.1 = (bf16[12,4,16384]{2,1,0:T(4,128)(2,1)}, bf16[4,8,16384]{2,1,0:T(8,128)(2,1)}) custom-call(s32[4]{0:T(128)} %length.1, bf16[2,32,48,256]{3,2,1,0:T(8,128)(2,1)} %get-tuple-element.6.values_p, bf16[2,32,32,256]{3,2,1,0:T(8,128)(2,1)} %get-tuple-element.7.values_o, f32[1,16384]{1,0:T(1,128)} %bitcast.11), custom_call_target="tpu_custom_call" | custom-call | tf_op jit(solution)/shard_map/norm/pallas_call | solution.py:655

commit v4 on v3

--- a/solution.py
+++ b/solution.py
@@ -38,7 +38,7 @@
     px, pbc, pg, pst, ox, obc, og, ost, xk, bck, sb, lr, sg,
     out_p, out_o,
     xpad, xpado, gp, go, rim, gat, states, dec, xs, ee, rows, bu, cu, scores, part, ybuf, ybufo,
-    pack_p, pack_o,
+    pack_p, pack_o, rest, gates, factors,
     load_sem, own_sem, rim_send, rim_recv, bc_send, bc_recv, ow_send, ow_recv, st_send, st_recv,
     dec_send, dec_recv, swap_send, swap_recv,
 ):
@@ -146,44 +146,42 @@
     bc_copy(1, 1, r, far).start()
     bc_copy(1, 0, r, near).start()
 
-    bias, rate = sb[...], -jnp.exp(lr[...])
+    same = lax.broadcasted_iota(jnp.int32, (8, 8), 0) == lax.broadcasted_iota(jnp.int32, (8, 8), 1)
+
+    def column(row):
+        grown = jnp.where(same, jnp.broadcast_to(row, (8, 8)), 0.0)
+        return jnp.concatenate([jnp.sum(grown, axis=1, keepdims=True)] * chunks, axis=0)
+
     raw = [pst[s, :, k * CHUNK : (k + 1) * CHUNK] for s in range(seqs) for k in range(pk)]
     raw += [ost[o, :, k * CHUNK : (k + 1) * CHUNK] for o in range(opts) for k in range(ok)]
-    raw += [jnp.zeros((256 - 8 * chunks, CHUNK), jnp.float32)]
-    raw = jnp.transpose(jnp.concatenate(raw, axis=0))
-    raw = raw + jnp.concatenate([bias] * 32, axis=1)
+    raw = jnp.concatenate(raw, axis=0) + column(sb[...])
     size = jnp.maximum(raw, 0.0) + jnp.log1p(jnp.exp(-jnp.abs(raw)))
-    move = size * jnp.concatenate([rate] * 32, axis=1)
+    move = size * column(-jnp.exp(lr[...]))
     across = lax.broadcasted_iota(jnp.int32, (CHUNK, CHUNK), 0)
     along = lax.broadcasted_iota(jnp.int32, (CHUNK, CHUNK), 1)
     lower = across >= along
-    cumul = dot(lower.astype(jnp.float32), move, precision=lax.Precision.HIGHEST)
-    middle, end = cumul[CHUNK // 2 - 1 : CHUNK // 2], cumul[CHUNK - 1 : CHUNK]
-    filler = jnp.zeros((13, end.shape[1]), jnp.float32)
-    wide = jnp.concatenate(
-        [
-            jnp.exp(middle - cumul) * size,
-            jnp.exp(cumul - middle),
-            jnp.exp(end),
-            jnp.exp(end - middle),
-            jnp.exp(middle),
-            filler,
-        ],
-        axis=0,
-    )
-    wide_high = wide.astype(jnp.bfloat16)
-    wide_low = (wide - wide_high.astype(jnp.float32)).astype(jnp.bfloat16)
-    lanes = wide.shape[1]
+    cumul = dot(move, (across <= along).astype(jnp.float32), precision=lax.Precision.HIGHEST)
+    middle, end = cumul[:, CHUNK // 2 - 1 : CHUNK // 2], cumul[:, CHUNK - 1 : CHUNK]
+    place = lax.broadcasted_iota(jnp.int32, cumul.shape, 1)
+    few = jnp.where(place == 0, end, jnp.where(place == 1, end - middle, middle))
+    wide = [jnp.exp(middle - cumul) * size, jnp.exp(cumul - middle), jnp.exp(few)]
+    for n in range(3):
+        at = slice(n * CHUNK, (n + 1) * CHUNK)
+        high = wide[n].astype(jnp.bfloat16).astype(jnp.float32)
+        factors[0, :, at] = high
+        factors[1, :, at] = wide[n] - high
     per_head = channels // 8
-    spread_row = lax.broadcasted_iota(jnp.int32, (lanes, channels), 0)
-    spread_head = lax.div(lax.broadcasted_iota(jnp.int32, (lanes, channels), 1), per_head)
+    pick = lax.broadcasted_iota(jnp.int32, (16, channels), 0)
+    pick = lax.rem(pick, 8) == lax.div(lax.broadcasted_iota(jnp.int32, (16, channels), 1), per_head)
+    pick = pick.astype(jnp.bfloat16)
 
     xtaps = xk[...].astype(jnp.float32)
 
     def convolve(j, window):
         out = conv_window(window, xtaps, CHUNK).astype(jnp.bfloat16)
-        pick = (spread_row == 8 * j + spread_head).astype(jnp.bfloat16)
-        grown = dot(wide_high, pick) + dot(wide_low, pick)
+        at = pl.multiple_of(8 * j, 8)
+        both = jnp.concatenate([factors[n, pl.ds(at, 8), :] for n in range(2)], axis=0)
+        grown = dot(jnp.transpose(both)[0 : 2 * CHUNK + 8].astype(jnp.bfloat16), pick)
         xs[j] = (out.astype(jnp.float32) * grown[0:CHUNK]).astype(jnp.bfloat16)
         ee[j] = grown[CHUNK : 2 * CHUNK]
         rows[j] = grown[2 * CHUNK : 2 * CHUNK + 8]
@@ -208,6 +206,8 @@
     def first_chunks(s, carry):
         prefix_conv(s, 0)
         return carry
+
+    lax.fori_loop(0, seqs * (pk - 1), later_chunks, 0)
 
     for d in range(1, 4):
         rim_copy(d, lax.rem(c + 4 - d, 4)).wait_recv()
@@ -239,13 +239,22 @@
     bc_copy(0, 1, r, far).start()
     bc_copy(0, 2, r, cross).start()
     bc_copy(0, 0, r, near).start()
-    bc_copy(2, 1, r, far).start()
-    bc_copy(2, 0, r, near).start()
-
-    lax.fori_loop(0, seqs * (pk - 1), later_chunks, 0)
-
-    bc_copy(1, 1, far_slot, far).wait_recv()
-    bc_copy(1, 2, far_slot, near).start()
+
+    def from_far():
+        bc_copy(1, 1, far_slot, far).wait_recv()
+        bc_copy(1, 2, far_slot, near).start()
+
+    def from_far_side():
+        bc_copy(0, 1, far_slot, far).wait_recv()
+        bc_copy(0, 2, cross_slot, cross).wait_recv()
+        bc_copy(1, 2, cross_slot, near).wait_recv()
+
+    def from_near():
+        bc_copy(0, 0, near_slot, near).wait_recv()
+        bc_copy(1, 0, near_slot, near).wait_recv()
+
+    has_b = r < 2
+    pl.when(jnp.logical_not(has_b))(from_far)
 
     lax.fori_loop(0, seqs, first_chunks, 0)
 
@@ -309,12 +318,11 @@
         scores[j] = jnp.where(lower, raw_scores, 0.0).astype(jnp.bfloat16)
         return carry
 
-    bc_copy(0, 0, near_slot, near).wait_recv()
-    bc_copy(0, 1, far_slot, far).wait_recv()
-    bc_copy(0, 2, cross_slot, cross).wait_recv()
-    bc_copy(1, 0, near_slot, near).wait_recv()
-    bc_copy(1, 2, cross_slot, near).wait_recv()
+    pl.when(has_b)(from_near)
+    pl.when(jnp.logical_not(has_b))(from_far_side)
     unfold_prefix(bu, 0)
+    bc_copy(2, 1, r, far).start()
+    bc_copy(2, 0, r, near).start()
 
     def owner_copy(d, side, s, slot):
         return ctx_copy(
@@ -337,8 +345,10 @@
             state = rows[j, 0:1, :] * state + rows[j, 1:2, :] * grown
         for side in range(2):
             states[c, side, s] = state[:, side * half : (side + 1) * half].astype(jnp.bfloat16)
-            if d < 4:
-                owner_copy(d, side, s, c).start()
+        if d < 4:
+            owner_copy(d, 0, s, c).start()
+    for d in range(1, 4):
+        owner_copy(d, 1, lax.rem(c + d, 4), c).start()
 
     for side in range(2):
         for d in range(1, 4):
@@ -348,15 +358,17 @@
                 for n in range(3):
                     state_copy(d, side, lax.rem(c + d + 1 + n, 4), c).start()
 
+    pl.when(has_b)(from_far)
+    lax.fori_loop(0, opts * ok, option_conv, 0)
     bc_copy(2, 1, far_slot, far).wait_recv()
     bc_copy(2, 2, far_slot, near).start()
-    lax.fori_loop(0, opts * ok, option_conv, 0)
+    pl.when(has_b)(from_far_side)
+    pl.when(jnp.logical_not(has_b))(from_near)
     bc_copy(2, 0, near_slot, near).wait_recv()
     bc_copy(2, 2, cross_slot, near).wait_recv()
     unfold_option(bu, 0)
     unfold_option(cu, 2)
-    unfold_prefix(cu, 2)
-    lax.fori_loop(0, chunks, score, 0)
+    lax.fori_loop(pchunks, chunks, score, 0)
 
     skip = sg[...]
     skip = dot(
@@ -375,6 +387,20 @@
     )
     skip = skip[0:1] + skip[1:2]
 
+    loads[3].wait()
+
+    def option_rest(at):
+        def one(i, carry):
+            o, k = i // ok, lax.rem(i, ok)
+            p = pl.multiple_of(k * CHUNK, CHUNK)
+            j = pchunks + i
+            x = xpado[o, pl.ds(p + HALO, CHUNK), at].astype(jnp.float32)
+            rest[i] = ee[j, :, at] * dot(scores[j], xs[j, :, at]) + skip[:, at] * x
+            gates[i] = silu(go[o, pl.ds(p, CHUNK), at].astype(jnp.float32))
+            return carry
+
+        lax.fori_loop(0, opts * ok, one, 0)
+
     def output(j, lo, state, x, gate):
         at = slice(lo, lo + half)
         entering = (state * rows[j, 2:3, at]).astype(jnp.bfloat16)
@@ -419,10 +445,10 @@
     for d in range(1, 4):
         dec_copy(d, lax.rem(c + 4 - d, 4)).wait_recv()
     loads[2].wait()
-    loads[3].wait()
     for side in range(2):
         lo = side * half
         at = slice(lo, lo + half)
+        option_rest(at)
         for d in range(1, 4):
             owner_copy(d, side, c, lax.rem(c + 4 - d, 4)).wait_recv()
         final = jnp.zeros((NS, half), jnp.float32)
@@ -437,9 +463,9 @@
                     grown = dot(bu[j - 1], xs[j - 1, :, at], ((0,), (0,)))
                     state = rows[j - 1, 0:1, at] * state + rows[j - 1, 1:2, at] * grown
                 p = k * CHUNK
-                m = output(
-                    j, lo, state, xpado[o, HALO + p : HALO + p + CHUNK, at], go[o, p : p + CHUNK, at]
-                )
+                entering = (state * rows[j, 2:3, at]).astype(jnp.bfloat16)
+                y = rest[o * ok + k] + ee[j, :, at] * dot(cu[j], entering)
+                m = y * gates[o * ok + k]
                 some = CHUNK // orr
                 ybufo[k * some : (k + 1) * some, pl.ds(pl.multiple_of(o * orr, 8), orr), :] = (
                     m.reshape(some, orr, half)
@@ -450,6 +476,9 @@
         for i in range(nh):
             pack_o[side, i] = ybufo[i].astype(jnp.bfloat16)
         send_all(0, side)
+
+    unfold_prefix(cu, 2)
+    lax.fori_loop(0, pchunks, score, 0)
 
     for side in range(2):
         lo = side * half
@@ -631,6 +660,9 @@
             pltpu.VMEM((nh, opts * orr, half), f32),
             pltpu.VMEM((2, nh, seqs * pr, half), bf16),
             pltpu.VMEM((2, nh, opts * orr, half), bf16),
+            pltpu.VMEM((opts * olen // CHUNK, CHUNK, half), f32),
+            pltpu.VMEM((opts * olen // CHUNK, CHUNK, half), f32),
+            pltpu.VMEM((2, 8 * chunks, 3 * CHUNK), f32),
             dma((4,)),
             dma((2, 2)),
             dma((1,)), dma((3,)),

time: 67.5 us -> 64.2 us (0.951)
  Pallas kernels: 66.6 us -> 63.3 us
    pallas_call x1, Pallas kernels: 62.1 us -> 58.8 us  [per_device(): pl.pallas_call(functools.partial(mixer_kernel, nh), out_shape=[jax.ShapeD...]
where the time goes in v4:
time: 64.2 us; the launch traced here: 64 us
  Pallas kernels  63.3 us (99%)
    pallas_call x1, Pallas kernels, per_device(): pl.pallas_call(functools.partial(mixer_kernel, nh), out_shape=[jax.ShapeD...  58.8 us
    pallas_call x1, Pallas kernels, per_device(): pl.pallas_call(functools.partial(norm_kernel, seqs, pr, opts, orr), in_sp...  4.52 us

profile of v4, /device:TPU:1, one launch (start us, length us, event | category | flops | bytes accessed | tf_op | source)
XLA Modules:
  0.0 64.0 jit_solution(15305399452208984509)
XLA Ops:
  0.6 58.8 %mixer.1 = (bf16[2,32,48,256]{3,2,1,0:T(8,128)(2,1)}, bf16[2,32,32,256]{3,2,1,0:T(8,128)(2,1)}) custom-call(bf16[4,384,512]{2,1,0:T(8,128)(2,1)} %px.1, bf16[4,64,384]{2,1,0:T(8,128)(2,1)} %bitcast.9, bf16[4,384,512]{2,1,0:T(8,128)(2,1)} %pg.1, f32[4,8,384]{2,1,0:T(8,128)} %bitcast.12, bf16[4,256,512]{2,1,0:T(8,128)(2,1)} %ox.1, ...), custom_call_target="tpu_custom_call" | custom-call | tf_op jit(solution)/shard_map/mixer/pallas_call | solution.py:635
  59.4 4.5 %norm.1 = (bf16[12,4,16384]{2,1,0:T(4,128)(2,1)}, bf16[4,8,16384]{2,1,0:T(8,128)(2,1)}) custom-call(s32[4]{0:T(128)} %length.1, bf16[2,32,48,256]{3,2,1,0:T(8,128)(2,1)} %get-tuple-element.6.values_p, bf16[2,32,32,256]{3,2,1,0:T(8,128)(2,1)} %get-tuple-element.7.values_o, f32[1,16384]{1,0:T(1,128)} %bitcast.11), custom_call_target="tpu_custom_call" | custom-call | tf_op jit(solution)/shard_map/norm/pallas_call | solution.py:687

commit v5 on v4

--- a/solution.py
+++ b/solution.py
@@ -35,10 +35,10 @@
 
 def mixer_kernel(
     heads,
-    px, pbc, pg, pst, ox, obc, og, ost, xk, bck, sb, lr, sg,
+    px, pbc, pg, pst, ox, obc, og, ost, xk, bck, sb, lr, sg, gain, length,
     out_p, out_o,
     xpad, xpado, gp, go, rim, gat, states, dec, xs, ee, rows, bu, cu, scores, part, ybuf, ybufo,
-    pack_p, pack_o, rest, gates, factors,
+    pack_p, pack_o, rest, gates, factors, got_o, res_o,
     load_sem, own_sem, rim_send, rim_recv, bc_send, bc_recv, ow_send, ow_recv, st_send, st_recv,
     dec_send, dec_recv, swap_send, swap_recv,
 ):
@@ -207,7 +207,7 @@
         prefix_conv(s, 0)
         return carry
 
-    lax.fori_loop(0, seqs * (pk - 1), later_chunks, 0)
+    lax.fori_loop(0, seqs * (pk - 1), later_chunks, 0, unroll=2)
 
     for d in range(1, 4):
         rim_copy(d, lax.rem(c + 4 - d, 4)).wait_recv()
@@ -256,7 +256,7 @@
     has_b = r < 2
     pl.when(jnp.logical_not(has_b))(from_far)
 
-    lax.fori_loop(0, seqs, first_chunks, 0)
+    lax.fori_loop(0, seqs, first_chunks, 0, unroll=2)
 
     for s in range(seqs):
         total = rows[s * pk, 0:1, :]
@@ -329,11 +329,6 @@
             states.at[slot, side, s], ow_send.at[0], ow_recv.at[d - 1, side], d
         )
 
-    def state_copy(d, side, s, slot):
-        return ctx_copy(
-            states.at[slot, side, s], st_send.at[d - 1], st_recv.at[d - 1, side], d
-        )
-
     for d in range(1, 5):
         s = lax.rem(c + d, 4)
         state = jnp.zeros((NS, channels), jnp.float32)
@@ -350,16 +345,19 @@
     for d in range(1, 4):
         owner_copy(d, 1, lax.rem(c + d, 4), c).start()
 
+    pl.when(has_b)(from_far)
+    lax.fori_loop(0, opts * ok, option_conv, 0, unroll=2)
     for side in range(2):
-        for d in range(1, 4):
-
-            @pl.when(c + d < 4)
+        for later in range(1, 4):
+
+            @pl.when(c < later)
             def _():
-                for n in range(3):
-                    state_copy(d, side, lax.rem(c + d + 1 + n, 4), c).start()
-
-    pl.when(has_b)(from_far)
-    lax.fori_loop(0, opts * ok, option_conv, 0)
+                d = later - c
+                for first, end_ in ((0, later), (later + 1, 4)):
+                    if first < end_:
+                        ref = states.at[c, side, pl.ds(first, end_ - first)]
+                        ctx_copy(ref, st_send.at[d - 1], st_recv.at[d - 1, side], d).start()
+
     bc_copy(2, 1, far_slot, far).wait_recv()
     bc_copy(2, 2, far_slot, near).start()
     pl.when(has_b)(from_far_side)
@@ -368,7 +366,7 @@
     bc_copy(2, 2, cross_slot, near).wait_recv()
     unfold_option(bu, 0)
     unfold_option(cu, 2)
-    lax.fori_loop(pchunks, chunks, score, 0)
+    lax.fori_loop(pchunks, chunks, score, 0, unroll=4)
 
     skip = sg[...]
     skip = dot(
@@ -399,7 +397,7 @@
             gates[i] = silu(go[o, pl.ds(p, CHUNK), at].astype(jnp.float32))
             return carry
 
-        lax.fori_loop(0, opts * ok, one, 0)
+        lax.fori_loop(0, opts * ok, one, 0, unroll=2)
 
     def output(j, lo, state, x, gate):
         at = slice(lo, lo + half)
@@ -411,7 +409,7 @@
     pr, orr = tokens // nh, olen // nh
 
     def swap_copy(kind, side, to):
-        packed, out = ((pack_o, out_o), (pack_p, out_p))[kind]
+        packed, out = ((pack_o, got_o), (pack_p, out_p))[kind]
         return pltpu.make_async_remote_copy(
             src_ref=packed.at[side, to], dst_ref=out.at[side, h],
             send_sem=swap_send.at[kind, side], recv_sem=swap_recv.at[kind, side],
@@ -419,7 +417,7 @@
         )
 
     def own_copy(kind, side):
-        packed, out = ((pack_o, out_o), (pack_p, out_p))[kind]
+        packed, out = ((pack_o, got_o), (pack_p, out_p))[kind]
         return pltpu.make_async_copy(packed.at[side, h], out.at[side, h], own_sem.at[kind, side])
 
     def send_all(kind, side):
@@ -431,7 +429,7 @@
         lax.fori_loop(1, nh, send, 0)
 
     def finish(kind, side):
-        packed, out = ((pack_o, out_o), (pack_p, out_p))[kind]
+        packed, out = ((pack_o, got_o), (pack_p, out_p))[kind]
         others = pl.ds(0, nh - 1)
         every = pltpu.make_async_remote_copy(
             src_ref=packed.at[side, others], dst_ref=out.at[side, others],
@@ -472,13 +470,13 @@
                 )
             return carry
 
-        lax.fori_loop(0, opts, option_out, 0)
+        lax.fori_loop(0, opts, option_out, 0, unroll=2)
         for i in range(nh):
             pack_o[side, i] = ybufo[i].astype(jnp.bfloat16)
         send_all(0, side)
 
     unfold_prefix(cu, 2)
-    lax.fori_loop(0, pchunks, score, 0)
+    lax.fori_loop(0, pchunks, score, 0, unroll=4)
 
     for side in range(2):
         lo = side * half
@@ -508,7 +506,7 @@
                 factor = factor * rows[j, 0:1, at]
             return carry
 
-        lax.fori_loop(0, seqs, prefix_out, 0)
+        lax.fori_loop(0, seqs, prefix_out, 0, unroll=2)
 
         def pack(i, carry, side=side):
             start = pl.multiple_of(i * seqs * pr, 16)
@@ -518,8 +516,33 @@
                 ].astype(jnp.bfloat16)
             return carry
 
-        lax.fori_loop(0, nh, pack, 0)
+        lax.fori_loop(0, nh, pack, 0, unroll=2)
         send_all(1, side)
+
+    for side in range(2):
+        finish(0, side)
+    place = lax.broadcasted_iota(jnp.int32, (orr, 1), 0) + h * orr
+    keep = [(place < length[o]).astype(jnp.float32) for o in range(opts)]
+    keep = jnp.concatenate(keep, axis=0)
+
+    def option_norm(group, carry):
+        squares = None
+        for i in range(4):
+            for side in range(2):
+                block = got_o[side, 4 * group + i].astype(jnp.float32)
+                squares = block * block if squares is None else squares + block * block
+        total = jnp.sum(squares, axis=1, keepdims=True)
+        scale = lax.rsqrt(total / (4 * channels) + EPSILON) * keep
+        for i in range(4):
+            for side in range(2):
+                at = pl.ds(pl.multiple_of((8 * group + 2 * i + side) * half, half), half)
+                out = got_o[side, 4 * group + i].astype(jnp.float32) * scale * gain[:, at]
+                res_o[:, :, at] = out.reshape(opts, orr, half).astype(jnp.bfloat16)
+        return carry
+
+    lax.fori_loop(0, nh // 4, option_norm, 0)
+    option_store = pltpu.make_async_copy(res_o, out_o, load_sem.at[0])
+    option_store.start()
 
     ctx_copy(rim.at[pl.ds(0, 3)], rim_send.at[0], rim_recv.at[0], 1).wait_send()
     ctx_copy(dec.at[pl.ds(0, 3)], dec_send.at[0], dec_recv.at[0], 1).wait_send()
@@ -536,70 +559,59 @@
         src_ref=some, dst_ref=some, send_sem=bc_send.at[0], recv_sem=bc_recv.at[0, 0],
         device_id=(c, near), device_id_type=MESH,
     ).wait_send()
-    for kind in range(2):
-        for side in range(2):
-            finish(kind, side)
+    for side in range(2):
+        finish(1, side)
+    option_store.wait()
 
 
 def norm_kernel(
-    seqs, pr, opts, orr, length, values_p, values_o, gain, prefix_out, option_out,
-    buf_p, buf_o, res_p, res_o, sems, out_sems,
+    seqs, pr, values, options, gain, prefix_out, option_out,
+    buf, row, res, held, sems, out_sems, rest_sems,
 ):
-    h = lax.axis_index("head")
-    half = values_p.shape[3]
-    groups = values_p.shape[1] // 4
+    half = values.shape[3]
+    groups = values.shape[1] // 4
     width = 8 * half
-    place = lax.broadcasted_iota(jnp.int32, (orr, 1), 0) + h * orr
-    keeps = [(place < length[o]).astype(jnp.float32) for o in range(opts)]
 
     def fetch(group):
         at = pl.ds(group * 4, 4)
-        return [
-            pltpu.make_async_copy(values.at[:, at], buf.at[:, at], sems.at[n, group])
-            for n, (values, buf) in enumerate(((values_p, buf_p), (values_o, buf_o)))
-        ]
+        return pltpu.make_async_copy(values.at[:, at], buf.at[:, at], sems.at[group])
 
     def store(group):
         at = pl.ds(group * width, width)
-        return [
-            pltpu.make_async_copy(res.at[:, :, at], out.at[:, :, at], out_sems.at[n, group])
-            for n, (res, out) in enumerate(((res_p, prefix_out), (res_o, option_out)))
-        ]
-
+        return pltpu.make_async_copy(
+            res.at[:, :, at], prefix_out.at[:, :, at], out_sems.at[group]
+        )
+
+    gain_copy = pltpu.make_async_copy(gain, row, rest_sems.at[0])
+    option_in = pltpu.make_async_copy(options, held, rest_sems.at[1])
+    option_copy = pltpu.make_async_copy(held, option_out, rest_sems.at[2])
+    gain_copy.start()
     for group in range(groups):
-        for copy in fetch(group):
-            copy.start()
-
-    def scale(buf, group):
+        fetch(group).start()
+    option_in.start()
+    gain_copy.wait()
+    for group in range(groups):
+        fetch(group).wait()
         squares = None
         for side in range(2):
             for i in range(4):
                 block = buf[side, group * 4 + i].astype(jnp.float32)
                 squares = block * block if squares is None else squares + block * block
         total = jnp.sum(squares, axis=1, keepdims=True)
-        return lax.rsqrt(total / (8 * half) + EPSILON)
-
-    for group in range(groups):
-        for copy in fetch(group):
-            copy.wait()
-        scale_p = scale(buf_p, group)
-        scale_o = scale(buf_o, group)
-        scale_o = jnp.concatenate(
-            [scale_o[o * orr : (o + 1) * orr] * keeps[o] for o in range(opts)], axis=0
-        )
+        scale = lax.rsqrt(total / width + EPSILON)
         for i in range(4):
             for side in range(2):
                 lo = (group * 8 + i * 2 + side) * half
                 at = slice(lo, lo + half)
-                out = buf_p[side, group * 4 + i].astype(jnp.float32) * scale_p * gain[:, at]
-                res_p[:, :, at] = out.reshape(pr, seqs, half).astype(jnp.bfloat16)
-                out = buf_o[side, group * 4 + i].astype(jnp.float32) * scale_o * gain[:, at]
-                res_o[:, :, at] = out.reshape(opts, orr, half).astype(jnp.bfloat16)
-        for copy in store(group):
-            copy.start()
+                out = buf[side, group * 4 + i].astype(jnp.float32) * scale * row[:, at]
+                res[:, :, at] = out.reshape(pr, seqs, half).astype(jnp.bfloat16)
+        store(group).start()
+        if group == groups // 2:
+            option_in.wait()
+            option_copy.start()
     for group in range(groups):
-        for copy in store(group):
-            copy.wait()
+        store(group).wait()
+    option_copy.wait()
 
 
 def per_device(
@@ -632,13 +644,18 @@
     dma = pltpu.SemaphoreType.DMA
     flip = functools.partial(jnp.swapaxes, axis1=1, axis2=2)
 
-    swapped_p, swapped_o = pl.pallas_call(
+    inner = nh * channels
+    gain = norm_gain.reshape(1, -1)
+
+    swapped, normed = pl.pallas_call(
         functools.partial(mixer_kernel, nh),
         out_shape=[
             jax.ShapeDtypeStruct((2, nh, seqs * pr, half), bf16),
-            jax.ShapeDtypeStruct((2, nh, opts * orr, half), bf16),
+            jax.ShapeDtypeStruct((opts, orr, inner), bf16),
         ],
-        in_specs=[anywhere, vmem, anywhere, vmem, anywhere, vmem, anywhere, vmem] + [vmem] * 5,
+        in_specs=[anywhere, vmem, anywhere, vmem, anywhere, vmem, anywhere, vmem]
+        + [vmem] * 6
+        + [pl.BlockSpec(memory_space=pltpu.SMEM)],
         out_specs=[anywhere, anywhere],
         scratch_shapes=[
             pltpu.VMEM((seqs, HALO + tokens, channels), bf16),
@@ -663,6 +680,8 @@
             pltpu.VMEM((opts * olen // CHUNK, CHUNK, half), f32),
             pltpu.VMEM((opts * olen // CHUNK, CHUNK, half), f32),
             pltpu.VMEM((2, 8 * chunks, 3 * CHUNK), f32),
+            pltpu.VMEM((2, nh, opts * orr, half), bf16),
+            pltpu.VMEM((opts, orr, inner), bf16),
             dma((4,)),
             dma((2, 2)),
             dma((1,)), dma((3,)),
@@ -681,20 +700,21 @@
         option_x, flip(option_bc), option_gate, flip(option_steps),
         x_kernel, bc_kernel,
         step_bias.reshape(1, -1), log_rate.reshape(1, -1), skip_gain.reshape(1, -1),
+        gain, option_len,
     )
 
-    inner = nh * channels
     prefix_out, option_out = pl.pallas_call(
-        functools.partial(norm_kernel, seqs, pr, opts, orr),
-        in_specs=[pl.BlockSpec(memory_space=pltpu.SMEM), anywhere, anywhere, vmem],
+        functools.partial(norm_kernel, seqs, pr),
+        in_specs=[anywhere] * 3,
         out_specs=[anywhere, anywhere],
         scratch_shapes=[
             pltpu.VMEM((2, nh, seqs * pr, half), bf16),
-            pltpu.VMEM((2, nh, opts * orr, half), bf16),
+            pltpu.VMEM((1, inner), f32),
             pltpu.VMEM((pr, seqs, inner), bf16),
             pltpu.VMEM((opts, orr, inner), bf16),
-            dma((2, nh // 4)),
-            dma((2, nh // 4)),
+            dma((nh // 4,)),
+            dma((nh // 4,)),
+            dma((3,)),
         ],
         out_shape=[
             jax.ShapeDtypeStruct((pr, seqs, inner), bf16),
@@ -702,7 +722,7 @@
         ],
         compiler_params=pltpu.CompilerParams(vmem_limit_bytes=60 * MIB),
         name="norm",
-    )(option_len, swapped_p, swapped_o, norm_gain.reshape(1, -1))
+    )(swapped, normed, gain)
     return jnp.swapaxes(prefix_out, 0, 1), option_out
 
 

time: 64.2 us -> 62.2 us (0.969)
  Pallas kernels: 63.3 us -> 60.9 us
    pallas_call x1, Pallas kernels: 58.8 us -> 57.4 us  [per_device(): pl.pallas_call(functools.partial(mixer_kernel, nh), out_shape=[jax.ShapeD...]
    pallas_call x1, Pallas kernels: 4.52 us -> 3.52 us  [per_device(): pl.pallas_call(functools.partial(norm_kernel, seqs, pr), in_specs=[anywhe...]
where the time goes in v5:
time: 62.2 us; the launch traced here: 61.6 us
  Pallas kernels  60.9 us (98%)
  between operations  0.64 us (1%)
    pallas_call x1, Pallas kernels, per_device(): pl.pallas_call(functools.partial(mixer_kernel, nh), out_shape=[jax.ShapeD...  57.4 us
    pallas_call x1, Pallas kernels, per_device(): pl.pallas_call(functools.partial(norm_kernel, seqs, pr), in_specs=[anywhe...  3.52 us

profile of v5, /device:TPU:1, one launch (start us, length us, event | category | flops | bytes accessed | tf_op | source)
XLA Modules:
  0.0 61.6 jit_solution(9626550315195991973)
XLA Ops:
  0.6 57.4 %mixer.1 = (bf16[2,32,48,256]{3,2,1,0:T(8,128)(2,1)}, bf16[4,8,16384]{2,1,0:T(8,128)(2,1)}) custom-call(bf16[4,384,512]{2,1,0:T(8,128)(2,1)} %px.1, bf16[4,64,384]{2,1,0:T(8,128)(2,1)} %bitcast.11, bf16[4,384,512]{2,1,0:T(8,128)(2,1)} %pg.1, f32[4,8,384]{2,1,0:T(8,128)} %bitcast.13, bf16[4,256,512]{2,1,0:T(8,128)(2,1)} %ox.1, bf16[4,64,256]{2,1,0:T(8,128)(2,1)} %bitcast.12, ...), custom_call_target="tpu_custom_call" | custom-call | tf_op jit(solution)/shard_map/mixer/pallas_call | solution.py:650
  58.1 3.5 %norm.1 = (bf16[12,4,16384]{2,1,0:T(4,128)(2,1)}, bf16[4,8,16384]{2,1,0:T(8,128)(2,1)}) custom-call(bf16[2,32,48,256]{3,2,1,0:T(8,128)(2,1)} %get-tuple-element.6.values, bf16[4,8,16384]{2,1,0:T(8,128)(2,1)} %get-tuple-element.7.options, f32[1,16384]{1,0:T(1,128)} %bitcast.10), custom_call_target="tpu_custom_call" | custom-call | tf_op jit(solution)/shard_map/norm/pallas_call | solution.py:706

commit v6 on v5

--- a/solution.py
+++ b/solution.py
@@ -35,10 +35,10 @@
 
 def mixer_kernel(
     heads,
-    px, pbc, pg, pst, ox, obc, og, ost, xk, bck, sb, lr, sg, gain, length,
+    px, pbc_in, pg, pst_in, ox, obc_in, og, ost_in, xk, bck, sb, lr, sg, gain_in, length,
     out_p, out_o,
     xpad, xpado, gp, go, rim, gat, states, dec, xs, ee, rows, bu, cu, scores, part, ybuf, ybufo,
-    pack_p, pack_o, rest, gates, factors, got_o, res_o,
+    pack_p, pack_o, rest, gates, factors, got_o, res_o, pbc, pst, obc, ost, gain,
     load_sem, own_sem, rim_send, rim_recv, bc_send, bc_recv, ow_send, ow_recv, st_send, st_recv,
     dec_send, dec_recv, swap_send, swap_recv,
 ):
@@ -49,7 +49,7 @@
     nh = heads
     pk, ok = tokens // CHUNK, olen // CHUNK
     pchunks, chunks = seqs * pk, seqs * pk + opts * ok
-    cols = pbc.shape[1]
+    cols = pbc_in.shape[1]
     half = channels // 2
     base = (h // 4) * 4
     r = lax.rem(h, 4)
@@ -64,6 +64,14 @@
     start_o = tops + seqs // 2 * long_p
     spans = ((0, tops), (tops, seqs // 2 * long_p), (start_o, opts // 2 * long_o))
 
+    narrow = [
+        pltpu.make_async_copy(source, target, load_sem.at[4 + n])
+        for n, (source, target) in enumerate(
+            ((pbc_in, pbc), (obc_in, obc), (pst_in, pst), (ost_in, ost), (gain_in, gain))
+        )
+    ]
+    for load in narrow:
+        load.start()
     loads = [
         pltpu.make_async_copy(px, xpad.at[:, pl.ds(HALO, tokens), :], load_sem.at[0]),
         pltpu.make_async_copy(ox, xpado.at[:, pl.ds(HALO, olen), :], load_sem.at[1]),
@@ -101,12 +109,14 @@
         return jnp.transpose(both.astype(jnp.float32))
 
     heads_p, heads_o, ends = [], [], []
+    narrow[0].wait()
     for a in range(seqs // 2):
         body = pair(pbc, a, seqs)
         heads_p.append(body[0:HALO])
         ends.append(body[tokens - 3 : tokens])
         out = conv_window(body, taps, long_p)
         gat[r, tops + a * long_p : tops + (a + 1) * long_p, :] = out.astype(jnp.bfloat16)
+    narrow[1].wait()
     for a in range(opts // 2):
         body = pair(obc, a, opts)
         heads_o.append(body[0:HALO])
@@ -152,6 +162,8 @@
         grown = jnp.where(same, jnp.broadcast_to(row, (8, 8)), 0.0)
         return jnp.concatenate([jnp.sum(grown, axis=1, keepdims=True)] * chunks, axis=0)
 
+    narrow[2].wait()
+    narrow[3].wait()
     raw = [pst[s, :, k * CHUNK : (k + 1) * CHUNK] for s in range(seqs) for k in range(pk)]
     raw += [ost[o, :, k * CHUNK : (k + 1) * CHUNK] for o in range(opts) for k in range(ok)]
     raw = jnp.concatenate(raw, axis=0) + column(sb[...])
@@ -177,14 +189,16 @@
 
     xtaps = xk[...].astype(jnp.float32)
 
-    def convolve(j, window):
-        out = conv_window(window, xtaps, CHUNK).astype(jnp.bfloat16)
+    every = slice(0, channels)
+
+    def convolve(j, window, cut=every):
+        out = conv_window(window, xtaps[:, cut], CHUNK).astype(jnp.bfloat16)
         at = pl.multiple_of(8 * j, 8)
         both = jnp.concatenate([factors[n, pl.ds(at, 8), :] for n in range(2)], axis=0)
-        grown = dot(jnp.transpose(both)[0 : 2 * CHUNK + 8].astype(jnp.bfloat16), pick)
-        xs[j] = (out.astype(jnp.float32) * grown[0:CHUNK]).astype(jnp.bfloat16)
-        ee[j] = grown[CHUNK : 2 * CHUNK]
-        rows[j] = grown[2 * CHUNK : 2 * CHUNK + 8]
+        grown = dot(jnp.transpose(both)[0 : 2 * CHUNK + 8].astype(jnp.bfloat16), pick[:, cut])
+        xs[j, :, cut] = (out.astype(jnp.float32) * grown[0:CHUNK]).astype(jnp.bfloat16)
+        ee[j, :, cut] = grown[CHUNK : 2 * CHUNK]
+        rows[j, :, cut] = grown[2 * CHUNK : 2 * CHUNK + 8]
         return out
 
     def prefix_conv(s, k):
@@ -192,12 +206,15 @@
         window = xpad[s, pl.ds(at, CHUNK + HALO), :].astype(jnp.float32)
         xpad[s, pl.ds(at + HALO, CHUNK), :] = convolve(s * pk + k, window)
 
-    def option_conv(i, carry):
-        o, k = i // ok, ok - 1 - lax.rem(i, ok)
-        at = pl.multiple_of(k * CHUNK, CHUNK)
-        window = xpado[o, pl.ds(at, CHUNK + HALO), :].astype(jnp.float32)
-        xpado[o, pl.ds(at + HALO, CHUNK), :] = convolve(pchunks + o * ok + k, window)
-        return carry
+    def option_conv(at):
+        def one(i, carry):
+            o, k = i // ok, ok - 1 - lax.rem(i, ok)
+            p = pl.multiple_of(k * CHUNK, CHUNK)
+            window = xpado[o, pl.ds(p, CHUNK + HALO), at].astype(jnp.float32)
+            xpado[o, pl.ds(p + HALO, CHUNK), at] = convolve(pchunks + o * ok + k, window, at)
+            return carry
+
+        lax.fori_loop(0, opts * ok, one, 0, unroll=2)
 
     def later_chunks(i, carry):
         prefix_conv(i // (pk - 1), pk - 1 - lax.rem(i, pk - 1))
@@ -346,7 +363,6 @@
         owner_copy(d, 1, lax.rem(c + d, 4), c).start()
 
     pl.when(has_b)(from_far)
-    lax.fori_loop(0, opts * ok, option_conv, 0, unroll=2)
     for side in range(2):
         for later in range(1, 4):
 
@@ -358,15 +374,12 @@
                         ref = states.at[c, side, pl.ds(first, end_ - first)]
                         ctx_copy(ref, st_send.at[d - 1], st_recv.at[d - 1, side], d).start()
 
-    bc_copy(2, 1, far_slot, far).wait_recv()
-    bc_copy(2, 2, far_slot, near).start()
+    @pl.when(c > 0)
+    def _():
+        option_conv(slice(0, half))
+
     pl.when(has_b)(from_far_side)
     pl.when(jnp.logical_not(has_b))(from_near)
-    bc_copy(2, 0, near_slot, near).wait_recv()
-    bc_copy(2, 2, cross_slot, near).wait_recv()
-    unfold_option(bu, 0)
-    unfold_option(cu, 2)
-    lax.fori_loop(pchunks, chunks, score, 0, unroll=4)
 
     skip = sg[...]
     skip = dot(
@@ -385,6 +398,7 @@
     )
     skip = skip[0:1] + skip[1:2]
 
+    loads[2].wait()
     loads[3].wait()
 
     def option_rest(at):
@@ -421,12 +435,25 @@
         return pltpu.make_async_copy(packed.at[side, h], out.at[side, h], own_sem.at[kind, side])
 
     def send_all(kind, side):
+        def fill(to):
+            if kind == 0:
+                pack_o[side, to] = ybufo[to].astype(jnp.bfloat16)
+                return
+            start = pl.multiple_of(to * seqs * pr, 16)
+            for n in range(half // 128):
+                pack_p[side, to, :, n * 128 : (n + 1) * 128] = ybuf[
+                    n, pl.ds(start, seqs * pr), :
+                ].astype(jnp.bfloat16)
+
         def send(i, carry):
-            swap_copy(kind, side, partner(i)).start()
+            to = partner(i)
+            fill(to)
+            swap_copy(kind, side, to).start()
             return carry
 
+        lax.fori_loop(1, nh, send, 0)
+        fill(h)
         own_copy(kind, side).start()
-        lax.fori_loop(1, nh, send, 0)
 
     def finish(kind, side):
         packed, out = ((pack_o, got_o), (pack_p, out_p))[kind]
@@ -440,12 +467,62 @@
         every.wait_send()
         every.wait_recv()
 
+    def prompts(alone):
+        unfold_prefix(cu, 2)
+        lax.fori_loop(0, pchunks, score, 0, unroll=4)
+
+        for side in range(2):
+            lo = side * half
+            at = slice(lo, lo + half)
+            for d in range(1, 1 if alone else 4):
+
+                @pl.when(c >= d)
+                def _():
+                    ref = states.at[lax.rem(c + 4 - d, 4), side, pl.ds(0, 3)]
+                    ctx_copy(ref, st_send.at[d - 1], st_recv.at[d - 1, side], d).wait_recv()
+
+            def prefix_out(s, carry, side=side, lo=lo, at=at):
+                state = jnp.zeros((NS, half), jnp.float32)
+                for i in range(0 if alone else 3):
+                    step = state * dec[i, pl.ds(s, 1), at] + states[i, side, s].astype(jnp.float32)
+                    state = jnp.where(i < c, step, state)
+                factor = jnp.ones((1, half), jnp.float32)
+                for k in range(pk):
+                    j = s * pk + k
+                    now = state if k == 0 else part[s * (pk - 1) + k - 1, :, at] + state * factor
+                    p = k * CHUNK
+                    m = output(
+                        j, lo, now, xpad[s, HALO + p : HALO + p + CHUNK, at], gp[s, p : p + CHUNK, at]
+                    )
+                    for n in range(half // 128):
+                        ybuf[n, pl.ds(seqs * p + s, CHUNK, seqs), :] = m[:, n * 128 : (n + 1) * 128]
+                    factor = factor * rows[j, 0:1, at]
+                return carry
+
+            lax.fori_loop(0, seqs, prefix_out, 0, unroll=2)
+
+            send_all(1, side)
+
+    @pl.when(c == 0)
+    def _():
+        prompts(True)
+        option_conv(slice(0, half))
+
+    bc_copy(2, 1, far_slot, far).wait_recv()
+    bc_copy(2, 2, far_slot, near).start()
+    bc_copy(2, 0, near_slot, near).wait_recv()
+    bc_copy(2, 2, cross_slot, near).wait_recv()
+    unfold_option(bu, 0)
+    unfold_option(cu, 2)
+    lax.fori_loop(pchunks, chunks, score, 0, unroll=4)
+
     for d in range(1, 4):
         dec_copy(d, lax.rem(c + 4 - d, 4)).wait_recv()
-    loads[2].wait()
     for side in range(2):
         lo = side * half
         at = slice(lo, lo + half)
+        if side == 1:
+            option_conv(at)
         option_rest(at)
         for d in range(1, 4):
             owner_copy(d, side, c, lax.rem(c + 4 - d, 4)).wait_recv()
@@ -471,54 +548,11 @@
             return carry
 
         lax.fori_loop(0, opts, option_out, 0, unroll=2)
-        for i in range(nh):
-            pack_o[side, i] = ybufo[i].astype(jnp.bfloat16)
         send_all(0, side)
 
-    unfold_prefix(cu, 2)
-    lax.fori_loop(0, pchunks, score, 0, unroll=4)
-
-    for side in range(2):
-        lo = side * half
-        at = slice(lo, lo + half)
-        for d in range(1, 4):
-
-            @pl.when(c >= d)
-            def _():
-                ref = states.at[lax.rem(c + 4 - d, 4), side, pl.ds(0, 3)]
-                ctx_copy(ref, st_send.at[d - 1], st_recv.at[d - 1, side], d).wait_recv()
-
-        def prefix_out(s, carry, side=side, lo=lo, at=at):
-            state = jnp.zeros((NS, half), jnp.float32)
-            for i in range(3):
-                step = state * dec[i, pl.ds(s, 1), at] + states[i, side, s].astype(jnp.float32)
-                state = jnp.where(i < c, step, state)
-            factor = jnp.ones((1, half), jnp.float32)
-            for k in range(pk):
-                j = s * pk + k
-                now = state if k == 0 else part[s * (pk - 1) + k - 1, :, at] + state * factor
-                p = k * CHUNK
-                m = output(
-                    j, lo, now, xpad[s, HALO + p : HALO + p + CHUNK, at], gp[s, p : p + CHUNK, at]
-                )
-                for n in range(half // 128):
-                    ybuf[n, pl.ds(seqs * p + s, CHUNK, seqs), :] = m[:, n * 128 : (n + 1) * 128]
-                factor = factor * rows[j, 0:1, at]
-            return carry
-
-        lax.fori_loop(0, seqs, prefix_out, 0, unroll=2)
-
-        def pack(i, carry, side=side):
-            start = pl.multiple_of(i * seqs * pr, 16)
-            for n in range(half // 128):
-                pack_p[side, i, :, n * 128 : (n + 1) * 128] = ybuf[
-                    n, pl.ds(start, seqs * pr), :
-                ].astype(jnp.bfloat16)
-            return carry
-
-        lax.fori_loop(0, nh, pack, 0, unroll=2)
-        send_all(1, side)
-
+    pl.when(c > 0)(functools.partial(prompts, False))
+
+    narrow[4].wait()
     for side in range(2):
         finish(0, side)
     place = lax.broadcasted_iota(jnp.int32, (orr, 1), 0) + h * orr
@@ -653,8 +687,9 @@
             jax.ShapeDtypeStruct((2, nh, seqs * pr, half), bf16),
             jax.ShapeDtypeStruct((opts, orr, inner), bf16),
         ],
-        in_specs=[anywhere, vmem, anywhere, vmem, anywhere, vmem, anywhere, vmem]
-        + [vmem] * 6
+        in_specs=[anywhere] * 8
+        + [vmem] * 5
+        + [anywhere]
         + [pl.BlockSpec(memory_space=pltpu.SMEM)],
         out_specs=[anywhere, anywhere],
         scratch_shapes=[
@@ -682,7 +717,12 @@
             pltpu.VMEM((2, 8 * chunks, 3 * CHUNK), f32),
             pltpu.VMEM((2, nh, opts * orr, half), bf16),
             pltpu.VMEM((opts, orr, inner), bf16),
-            dma((4,)),
+            pltpu.VMEM((seqs, prefix_bc.shape[2], tokens), bf16),
+            pltpu.VMEM((seqs, prefix_steps.shape[2], tokens), f32),
+            pltpu.VMEM((opts, option_bc.shape[2], olen), bf16),
+            pltpu.VMEM((opts, option_steps.shape[2], olen), f32),
+            pltpu.VMEM((1, inner), f32),
+            dma((9,)),
             dma((2, 2)),
             dma((1,)), dma((3,)),
             dma((1,)), dma((3, 3)),

time: 62.2 us -> 61.8 us (level)
  the two profiles are of different devices: /device:TPU:1 before, /device:TPU:7 now
where the time goes in v6:
time: 61.8 us; the launch traced here: 61.6 us
  Pallas kernels  60.9 us (99%)
  between operations  0.64 us (1%)
    pallas_call x1, Pallas kernels, per_device(): pl.pallas_call(functools.partial(mixer_kernel, nh), out_shape=[jax.ShapeD...  57.4 us
    pallas_call x1, Pallas kernels, per_device(): pl.pallas_call(functools.partial(norm_kernel, seqs, pr), in_specs=[anywhe...  3.52 us

profile of v6, /device:TPU:7, one launch (start us, length us, event | category | flops | bytes accessed | tf_op | source)
XLA Modules:
  0.0 61.6 jit_solution(9261343111708062424)
XLA Ops:
  0.6 57.4 %mixer.1 = (bf16[2,32,48,256]{3,2,1,0:T(8,128)(2,1)}, bf16[4,8,16384]{2,1,0:T(8,128)(2,1)}) custom-call(bf16[4,384,512]{2,1,0:T(8,128)(2,1)} %px.1, bf16[4,64,384]{2,1,0:T(8,128)(2,1)} %bitcast.11, bf16[4,384,512]{2,1,0:T(8,128)(2,1)} %pg.1, f32[4,8,384]{2,1,0:T(8,128)} %bitcast.13, bf16[4,256,512]{2,1,0:T(8,128)(2,1)} %ox.1, bf16[4,64,256]{2,1,0:T(8,128)(2,1)} %bitcast.12, ...), custom_call_target="tpu_custom_call" | custom-call | tf_op jit(solution)/shard_map/mixer/pallas_call | solution.py:684
  58.1 3.5 %norm.1 = (bf16[12,4,16384]{2,1,0:T(4,128)(2,1)}, bf16[4,8,16384]{2,1,0:T(8,128)(2,1)}) custom-call(bf16[2,32,48,256]{3,2,1,0:T(8,128)(2,1)} %get-tuple-element.6.values, bf16[4,8,16384]{2,1,0:T(8,128)(2,1)} %get-tuple-element.7.options, f32[1,16384]{1,0:T(1,128)} %bitcast.10), custom_call_target="tpu_custom_call" | custom-call | tf_op jit(solution)/shard_map/norm/pallas_call | solution.py:746
